TPU v7x, 256 devices: a whole 4x4x8 slice. The times are simulated.
256 devices in a mesh: row: 32 (over x_lo, z, core), col: 8 (over y, x_hi).
Axes of the slice: x: 4 (x_hi: 2, x_lo: 2; x = x_hi * 2 + x_lo), y: 4, z: 8, core: 2. Of those that a mesh axis runs over, the one named last changes fastest.
Arguments:
- tokens: bfloat16 [512, 12288], P('row', 'col'), may hold values from -6 to 6
- cotangent: bfloat16 [512, 12288], P('row', 'col'), may hold values from -40 to 40
- up_weight: bfloat16 [12288, 24576], P('col', 'row'), may hold values from -0.078125 to 0.078125
- down_weight: bfloat16 [24576, 12288], P('row', 'col'), may hold values from -0.0546875 to 0.0546875
- up_keep: int32 [96, 192], P('col', 'row'), may hold values 0 or 1
- down_keep: int32 [192, 96], P('row', 'col'), may hold values 0 or 1
- clip_norms: int32 [4], replicated, may hold values from 200 to 1999
Outputs:
- output: bfloat16 [512, 12288], P('row', 'col')
- input_grad: bfloat16 [512, 12288], P('row', 'col')
- up_update: bfloat16 [12288, 24576], P('col', 'row')
- down_update: bfloat16 [24576, 12288], P('row', 'col')
All inputs are finite; a program needn't handle non-finite values. No bound on the sum of `up_keep` or of `down_keep` on one device may be relied on, other than what follows from the above.
Results may differ from a plain program's by a relative error of at most 0.0056.
Values may be sent and summed in bfloat16 or wider, within the bound.
A program may use at most 64 MiB of HBM per device.

v0:
```python
import math

import jax
import jax.numpy as jnp
from jax import lax
from jax.sharding import PartitionSpec as P

D = 12288
FF = 24576
SEQ = 128


def gelu_tanh(value):
    return jax.nn.gelu(value, approximate=True)


def block_mask(keep, rows, cols, dtype):
    nrow, ncol = keep.shape
    side_r = rows // nrow
    side_c = cols // ncol
    spread = jnp.broadcast_to(keep.astype(dtype)[:, None, :, None], (nrow, side_r, ncol, side_c))
    return spread.reshape(rows, cols)


def local(tokens, cotangent, up_weight, down_weight, up_keep, down_keep, clip_norms):
    up_mask = block_mask(up_keep, up_weight.shape[0], up_weight.shape[1], jnp.bfloat16)
    down_mask = block_mask(down_keep, down_weight.shape[0], down_weight.shape[1], jnp.bfloat16)
    up_tile = up_weight * up_mask
    down_tile = down_weight * down_mask
    token_panel = lax.all_gather(tokens, "row", axis=0, tiled=True)
    partial_pre = jnp.dot(token_panel, up_tile, preferred_element_type=jnp.float32)
    cot_panel = lax.all_gather(cotangent, "row", axis=0, tiled=True)
    pre_part = lax.psum_scatter(partial_pre, "col", scatter_dimension=0, tiled=True)
    act_part, back_part = jax.vjp(gelu_tanh, pre_part)
    hidden = lax.all_gather(act_part.astype(jnp.bfloat16), "col", axis=0, tiled=True)
    block_rows = hidden
    output = lax.psum_scatter(
        jnp.dot(block_rows, down_tile, preferred_element_type=jnp.float32),
        "row",
        scatter_dimension=0,
        tiled=True,
    ).astype(jnp.bfloat16)
    partial_grad = lax.dot_general(
        cot_panel, down_tile, (((1,), (1,)), ((), ())), preferred_element_type=jnp.float32
    )
    grad_part = lax.psum_scatter(partial_grad, "col", scatter_dimension=0, tiled=True)
    pre_grad_part = back_part(grad_part)[0].astype(jnp.bfloat16)
    pre_grad = lax.all_gather(pre_grad_part, "col", axis=0, tiled=True)
    block_rows = pre_grad
    input_grad = lax.psum_scatter(
        lax.dot_general(
            block_rows, up_tile, (((1,), (1,)), ((), ())), preferred_element_type=jnp.float32
        ),
        "row",
        scatter_dimension=0,
        tiled=True,
    ).astype(jnp.bfloat16)
    examples = clip_norms.shape[0]
    seq_len = token_panel.shape[0] // examples
    up_each = jnp.einsum(
        "etd,etf->edf",
        token_panel.reshape(examples, seq_len, -1),
        pre_grad.reshape(examples, seq_len, -1),
        preferred_element_type=jnp.float32,
    )
    up_each = up_each * up_mask[None]
    down_each = jnp.einsum(
        "etf,etd->efd",
        hidden.reshape(examples, seq_len, -1),
        cot_panel.reshape(examples, seq_len, -1),
        preferred_element_type=jnp.float32,
    )
    down_each = down_each * down_mask[None]
    local_squares = jnp.sum(up_each * up_each, axis=(1, 2)) + jnp.sum(
        down_each * down_each, axis=(1, 2)
    )
    squared = lax.psum(local_squares, ("row", "col"))
    bound = clip_norms.astype(jnp.float32) * (math.sqrt(D * FF * SEQ) / 1000.0)
    factor = jnp.minimum(jnp.float32(1.0), bound / jnp.sqrt(squared + 1e-06))
    row_factor = jnp.repeat(factor, seq_len)[:, None]
    pre_scaled = (pre_grad.astype(jnp.float32) * row_factor).astype(jnp.bfloat16)
    cot_scaled = (cot_panel.astype(jnp.float32) * row_factor).astype(jnp.bfloat16)
    unit = 7.0 / (examples * math.sqrt(SEQ))
    up_sum = lax.dot_general(
        token_panel, pre_scaled, (((0,), (0,)), ((), ())), preferred_element_type=jnp.float32
    )
    up_update = (up_sum * up_mask * unit).astype(jnp.bfloat16)
    down_sum = lax.dot_general(
        hidden, cot_scaled, (((0,), (0,)), ((), ())), preferred_element_type=jnp.float32
    )
    down_update = (down_sum * down_mask * unit).astype(jnp.bfloat16)
    return (output, input_grad, up_update, down_update)


def solution(mesh):
    placed = (
        P("row", "col"),
        P("row", "col"),
        P("col", "row"),
        P("row", "col"),
        P("col", "row"),
        P("row", "col"),
        P(),
    )
    return jax.shard_map(
        local,
        mesh=mesh,
        in_specs=placed,
        out_specs=(P("row", "col"), P("row", "col"), P("col", "row"), P("row", "col")),
        check_vma=False,
    )
```

profile of v0, /device:TPU:1, one launch (start us, length us, event | category | flops | bytes accessed | tf_op | source)
XLA Modules:
  0.0 593.9 jit_solution(13799188083715987418)
XLA Ops:
  7.2 0.7 all-gather.3.cloned.1.call-update
  7.9 0.7 all-gather.5.cloned.1.call-update
  8.7 0.7 convert_element_type.57
  10.0 1.2 copy-done
  11.2 2.5 fusion.14
  13.7 64.7 %all-gather.3.cloned.1.call-done = bf16[512,1536]{1,0:T(8,128)(2,1)} async-done(((bf16[16,1536]{1,0:T(8,128)(2,1)}), bf16[512,1536]{1,0:T(8,128)(2,1)}) %all-gather.3.cloned.1.call-update) | async-done | bytes 1572880 | tf_op jit(solution)/shard_map/all_gather | solution.py:30
  78.4 3.5 convolution_bitcast_fusion.1
  82.0 1.6 copy.47
  83.7 60.6 %all-gather.5.cloned.1.call-done = bf16[512,1536]{1,0:T(8,128)(2,1)} async-done(((bf16[16,1536]{1,0:T(8,128)(2,1)}), bf16[512,1536]{1,0:T(8,128)(2,1)}) %all-gather.5.cloned.1.call-update) | async-done | bytes 1572880 | tf_op jit(solution)/shard_map/all_gather | solution.py:32
  144.7 0.9 copy-done.7
  145.7 4.3 convolution_bitcast_fusion
  149.9 3.0 copy.49
  153.0 71.5 %reduce-scatter.13.cloned.1.call-done = f32[64,768]{1,0:T(8,128)} async-done(((f32[512,768]{1,0:T(8,128)}), f32[64,768]{1,0:T(8,128)}) %reduce-scatter.13.cloned.1.call-update) | async-done | bytes 196624 | tf_op jit(solution)/shard_map/reduce_scatter | solution.py:33
  224.5 81.4 %reduce-scatter.15.cloned.1.call-done = f32[64,768]{1,0:T(8,128)} async-done(((f32[512,768]{1,0:T(8,128)}), f32[64,768]{1,0:T(8,128)}) %reduce-scatter.15.cloned.1.call-update) | async-done | bytes 196624 | tf_op jit(solution)/shard_map/reduce_scatter | solution.py:46
  305.9 1.2 fusion.13
  307.1 32.2 %all_gather.15 = bf16[512,768]{1,0:T(8,128)(2,1)S(1)} all-gather(bf16[64,768]{1,0:T(8,128)(2,1)S(1)} %get-tuple-element.26), channel_id=1, replica_groups=mesh['row'=32,'col'=8] {'col'}, dimensions={0}, use_global_device_ids=true | all-gather | bytes 884736 | tf_op jit(solution)/shard_map/all_gather | solution.py:48
  339.3 0.9 copy-done.1
  340.1 4.7 fusion.15
  344.9 32.3 %all_gather.13 = bf16[512,768]{1,0:T(8,128)(2,1)S(1)} all-gather(bf16[64,768]{1,0:T(8,128)(2,1)S(1)} %get-tuple-element.27), channel_id=1, replica_groups=mesh['row'=32,'col'=8] {'col'}, dimensions={0}, use_global_device_ids=true | all-gather | bytes 884736 | tf_op jit(solution)/shard_map/all_gather | solution.py:35
  377.2 0.9 copy-done.3
  378.2 4.8 fusion.6
  383.0 4.3 copy.42
  387.3 2.3 convert_element_type.65
  391.3 4.2 multiply_reduce_fusion
  395.5 4.2 fusion.1
  399.7 85.5 %psum.7 = f32[4]{0:T(128)S(1)} all-reduce(f32[4]{0:T(128)S(1)} %add.25), channel_id=1, replica_groups=mesh['row'=32,'col'=8] {'row','col'}, use_global_device_ids=true, to_apply=%region_6.0 | all-reduce | flops 4 | bytes 32 | tf_op jit(solution)/shard_map/psum | solution.py:77
  485.3 5.3 fusion.3
  490.7 4.3 copy.44
  494.9 4.8 multiply_convert_fusion
  499.7 1.5 convert_element_type.62
  501.2 84.3 %reduce-scatter.9.cloned.1.call-done = f32[16,1536]{1,0:T(8,128)} async-done(((f32[512,1536]{1,0:T(8,128)}), f32[16,1536]{1,0:T(8,128)}) %reduce-scatter.9.cloned.1.call-update) | async-done | bytes 98320 | tf_op jit(solution)/shard_map/reduce_scatter | solution.py:37
  585.5 1.5 convert_element_type.60
  (35 shorter events, 3.1 us)
Async XLA Ops:
  7.2 71.2 %all-gather.3.cloned.1.call-start = ((), (), s32[]{:S(2)}) async-start(), calls=%async_computation.4 | async-start | bytes 1622016 | tf_op jit(solution)/shard_map/all_gather | solution.py:30
  7.9 136.3 %all-gather.5.cloned.1.call-start = ((), (), s32[]{:S(2)}) async-start(), calls=%async_computation.6 | async-start | bytes 1622016 | tf_op jit(solution)/shard_map/all_gather | solution.py:32
  8.7 215.9 %reduce-scatter.13.cloned.1.call-start = ((), (), s32[]{:S(2)}) async-start(), calls=%async_computation.8 | async-start | bytes 1769472 | tf_op jit(solution)/shard_map/reduce_scatter | solution.py:33
  9.5 1.7 copy-start
  82.0 1.7 copy-start.5
  83.6 222.3 %reduce-scatter.15.cloned.1.call-start = ((), (), s32[]{:S(2)}) async-start(), calls=%async_computation.9 | async-start | bytes 1769472 | tf_op jit(solution)/shard_map/reduce_scatter | solution.py:46
  144.2 1.4 copy-start.7
  153.0 346.7 %reduce-scatter.11.cloned.1.call-start = ((), (), s32[]{:S(2)}) async-start(), calls=%async_computation.7 | async-start | bytes 3244032 | tf_op jit(solution)/shard_map/reduce_scatter | solution.py:50
  339.3 0.9 copy-start.1
  344.9 240.6 %reduce-scatter.9.cloned.1.call-start = ((), (), s32[]{:S(2)}) async-start(), calls=%async_computation.5 | async-start | bytes 3244032 | tf_op jit(solution)/shard_map/reduce_scatter | solution.py:37
  377.2 0.9 copy-start.3
  389.6 1.1 copy-start.4
  389.6 1.7 copy-start.8
  391.3 4.2 copy-start.2
  391.3 4.2 copy-start.6
  395.5 89.8 %copy-start.9 = (s32[4]{0:T(128)S(1)}, s32[4]{0:T(128)}, u32[]{:S(2)}) copy-start(s32[4]{0:T(128)} %param.13) | copy-start | bytes 52
Sparse Core Ops, SparseCore 0:
  9.9 68.5 all-gather.2
  80.3 63.9 all-gather.4
  148.2 76.2 reduce-scatter.12
  228.9 77.0 reduce-scatter.14
  345.0 122.0 reduce-scatter.10
  469.7 115.7 reduce-scatter.8
where the time goes:
time: 598 us; the launch traced here: 594 us
  waiting for transfers between devices  364 us (61%)
  blocking collectives  150 us (25%)
  matrix products  35.9 us (6%)
  local copies, waits for them, and re-layouts  19.3 us (3%)
  between operations  14.2 us (2%)
  other arithmetic  10.3 us (2%)
    psum x1, blocking collectives, local(): squared = lax.psum(local_squares, ('row', 'col'))  85.5 us
    reduce_scatter x1, waiting for transfers between devices, local(): lax.psum_scatter(jnp.dot(block_rows, down_tile, preferred_element_type=jn...  84.3 us
    reduce_scatter x1, waiting for transfers between devices, local(): lax.psum_scatter(partial_grad, 'col', scatter_dimension=0, tiled=True)  81.4 us
    reduce_scatter x1, waiting for transfers between devices, local(): lax.psum_scatter(partial_pre, 'col', scatter_dimension=0, tiled=True)  71.5 us
    all_gather x1, waiting for transfers between devices, local(): token_panel = lax.all_gather(tokens, 'row', axis=0, tiled=True)  64.7 us
    all_gather x1, waiting for transfers between devices, local(): cot_panel = lax.all_gather(cotangent, 'row', axis=0, tiled=True)  60.6 us
    all_gather x1, blocking collectives, local(): lax.all_gather(act_part.astype(jnp.bfloat16), 'col', axis=0, tiled=True)  32.3 us
    all_gather x1, blocking collectives, local(): pre_grad = lax.all_gather(pre_grad_part, 'col', axis=0, tiled=True)  32.2 us
  transfers between devices with their start and end apart: 6, of which 5 were waited for; matrix products, arithmetic and copies ran while one was open for 9% of the time, Pallas kernels for 0%

commit v1 on v0

v1 whole, which is shorter than its diff:
```python
import functools
import math

import jax
import jax.numpy as jnp
from jax import lax
from jax.experimental import pallas as pl
from jax.experimental.pallas import tpu as pltpu
from jax.sharding import PartitionSpec as P

MESH = pl.DeviceIdType.MESH
D = 12288
FF = 24576
SEQ = 128
BLK = 128
EX = 4
SUB = 16
F32 = jnp.float32
BF16 = jnp.bfloat16
ROOT = math.sqrt(2.0 / math.pi)
UNIT = 7.0 / (EX * math.sqrt(SEQ))
BOUND = math.sqrt(D * FF * SEQ) / 1000.0


def dot(a, b, ca, cb):
    return lax.dot_general(a, b, (((ca,), (cb,)), ((), ())), preferred_element_type=F32)


def kernel(
    nz, nc,
    tok, cot, up, dn, upk, dnk, clip,
    out_o, ing_o, up_o, dn_o,
    tokp, cotp, upm, dnm, mu, md,
    send_h, recv_h, hid, pg, dact,
    part, pair, pair_r, ring_s, ring_r, fin, fin_s, fin_r,
    sq_a, sq_s, sq_r, psc, csc, uo, do,
    loc_sem, ag_s, ag_r, col_s, col_r, row_s, row_r, sq_ss, sq_rs,
):
    tokens = tok.shape[0] * 4 * nz
    width = tok.shape[1]
    hidden = up.shape[1]
    r = lax.axis_index("row")
    c = lax.axis_index("col")
    core = lax.rem(r, 2)
    z = lax.rem(lax.div(r, 2), nz)
    x = lax.div(r, 2 * nz)

    def row_of(xx, zz, kk):
        return (xx * nz + zz) * 2 + kk

    def zmod(v):
        return lax.rem(v + 2 * nz, nz)

    me = (r, c)
    core_dev = (row_of(x, z, 1 - core), c)
    x_dev = (row_of(1 - x, z, core), c)
    xc_dev = (row_of(1 - x, z, 1 - core), c)
    z_dev = [(row_of(x, zmod(z + 1), core), c), (row_of(x, zmod(z - 1), core), c)]

    def z_at(k):
        return (row_of(x, zmod(z + k), core), c)

    def c_at(k):
        return (r, lax.rem(c + k, nc))

    up_in = pltpu.make_async_copy(up, upm, loc_sem.at[0])
    dn_in = pltpu.make_async_copy(dn, dnm, loc_sem.at[1])
    up_in.start()
    dn_in.start()

    def rows(ref, xx, zz, kk):
        return ref.at[pl.ds(pl.multiple_of(row_of(xx, zz, kk) * SUB, SUB), SUB)]

    own = [
        pltpu.make_async_copy(tok, rows(tokp, x, z, core), loc_sem.at[2]),
        pltpu.make_async_copy(cot, rows(cotp, x, z, core), loc_sem.at[3]),
    ]
    own[0].start()
    own[1].start()

    barrier = pltpu.get_barrier_semaphore()
    peers = [core_dev, x_dev, xc_dev]
    peers += [z_at(k) for k in range(1, nz)]
    peers += [c_at(k) for k in range(1, nc)]
    for dev in peers:
        pl.semaphore_signal(barrier, inc=1, device_id=dev, device_id_type=MESH)
    pl.semaphore_wait(barrier, len(peers))

    pending = []

    def send(src, dst, ssem, rsem, dev):
        copy = pltpu.make_async_remote_copy(
            src_ref=src, dst_ref=dst, send_sem=ssem, recv_sem=rsem, device_id=dev, device_id_type=MESH
        )
        copy.start()
        pending.append(copy)
        return copy

    def arrived(dst, rsem, dev):
        pltpu.make_async_remote_copy(
            src_ref=dst, dst_ref=dst, send_sem=rsem, recv_sem=rsem, device_id=dev, device_id_type=MESH
        ).wait_recv()

    half = nz // 2
    reach = [[half, half - 1], [half - 1, half]]
    n_ring = 4 * half

    def ring_id(stream, way, step):
        return 1 + (stream * 2 + way) * half + step

    core_base = 1 + n_ring

    class Gather:
        def __init__(self, a, shard, panel):
            self.a, self.shard, self.panel = a, shard, panel

        def sems(self, k):
            return ag_s.at[self.a, k], ag_r.at[self.a, k]

        def slot(self, stream, off):
            xx = x if stream == 0 else 1 - x
            return rows(self.panel, xx, zmod(z + off), core)

        def to_core(self, stream, off, src=None):
            dst = self.slot(stream, off)
            k = core_base + stream * nz + (off % nz)
            send(dst if src is None else src, dst, *self.sems(k), core_dev)

        def start(self):
            dst = self.slot(0, 0)
            send(self.shard, dst, *self.sems(0), x_dev)
            for way in (0, 1):
                send(self.shard, dst, *self.sems(ring_id(0, way, 0)), z_dev[way])
            self.to_core(0, 0, self.shard)

        def start_partner(self):
            dst = self.slot(1, 0)
            arrived(dst, self.sems(0)[1], x_dev)
            for way in (0, 1):
                send(dst, dst, *self.sems(ring_id(1, way, 0)), z_dev[way])
            self.to_core(1, 0)

        def step(self, s):
            for stream in (0, 1):
                for way in (0, 1):
                    if s - 1 >= reach[stream][way]:
                        continue
                    off = -s if way == 0 else s
                    src = self.slot(stream, off)
                    arrived(src, self.sems(ring_id(stream, way, s - 1))[1], z_dev[1 - way])
                    if s < reach[stream][way]:
                        send(src, src, *self.sems(ring_id(stream, way, s)), z_dev[way])
                    self.to_core(stream, off)

        def finish(self):
            for stream in (0, 1):
                for off in range(nz):
                    xx = x if stream == 0 else 1 - x
                    dst = rows(self.panel, xx, zmod(z + off), 1 - core)
                    arrived(dst, self.sems(core_base + stream * nz + off)[1], core_dev)

    gt = Gather(0, tok, tokp)
    gc = Gather(1, cot, cotp)
    gt.start()
    gt.start_partner()
    gt.step(1)
    gt.step(2)
    gc.start()
    gc.start_partner()

    nbu, nbh = width // BLK, hidden // BLK
    for i in range(nbu):
        for j in range(nbh):
            mu[i : i + 1, j * BLK : (j + 1) * BLK] = jnp.full((1, BLK), upk[i, j].astype(F32))
            md[j : j + 1, i * BLK : (i + 1) * BLK] = jnp.full((1, BLK), dnk[j, i].astype(F32))
    up_in.wait()

    @pl.loop(0, nbu)
    def _(i):
        at = pl.ds(pl.multiple_of(i * BLK, BLK), BLK)
        upm[at, :] = upm[at, :] * mu[pl.ds(i, 1), :].astype(BF16)

    gt.step(3)
    dn_in.wait()

    @pl.loop(0, nbh)
    def _(j):
        at = pl.ds(pl.multiple_of(j * BLK, BLK), BLK)
        dnm[at, :] = dnm[at, :] * md[pl.ds(j, 1), :].astype(BF16)

    for s in range(4, half + 1):
        gt.step(s)
    own[0].wait()
    gt.finish()

    blk = tokens // nc
    chunk = 256
    per = chunk // blk
    n_chunk = tokens // chunk

    def col_send(a, src, dst, q, k):
        return send(src, dst, col_s.at[a, k], col_r.at[a, k], (r, q))

    def scatter_chunk(a, m, value):
        for b in range(per):
            send_h[a, m * per + b] = value[b * blk : (b + 1) * blk].astype(BF16)

    def scatter_send(a):
        for k in range(1, nc):
            q = lax.rem(c + k, nc)
            col_send(a, send_h.at[a, q], recv_h.at[a, k], q, k)

    def scatter_sum(a):
        total = send_h[a, c].astype(F32)
        for k in range(1, nc):
            arrived(recv_h.at[a, k], col_r.at[a, k], c_at(nc - k))
            total += recv_h[a, k].astype(F32)
        return total

    def gather_send(a, panel):
        for k in range(1, nc):
            col_send(a, panel.at[c], panel.at[c], lax.rem(c + k, nc), k)

    def gather_wait(a, panel):
        for k in range(1, nc):
            q = lax.rem(c + nc - k, nc)
            arrived(panel.at[q], col_r.at[a, k], (r, q))

    for m in range(n_chunk):
        scatter_chunk(0, m, dot(tokp[m * chunk : (m + 1) * chunk], upm[...], 1, 0))
    scatter_send(0)

    for s in range(1, half + 1):
        gc.step(s)
    own[1].wait()
    gc.finish()

    for m in range(n_chunk):
        scatter_chunk(1, m, dot(cotp[m * chunk : (m + 1) * chunk], dnm[...], 1, 1))

    v = scatter_sum(0)
    t = jnp.tanh(ROOT * (v + 0.044715 * (v * v * v)))
    hid[c] = (0.5 * v * (1.0 + t)).astype(BF16)
    gather_send(2, hid)
    dact[...] = 0.5 * (1.0 + t) + (0.5 * ROOT) * v * (1.0 - t * t) * (1.0 + 0.134145 * (v * v))
    scatter_send(1)

    g = scatter_sum(1)
    pg[c] = (g * dact[...]).astype(BF16)
    gather_send(3, pg)

    class RowSum:
        def __init__(self, a):
            self.a = a

        def sems(self, k):
            return row_s.at[self.a, k], row_r.at[self.a, k]

        def rows_of(self, m, value):
            v4 = value.reshape(nz, 2, SUB, width)
            part[0, m] = v4[:, 0]
            part[1, m] = v4[:, 1]
            pair[self.a, 0, m] = v4[:, 0].astype(BF16)
            pair[self.a, 1, m] = v4[:, 1].astype(BF16)
            send(pair.at[self.a, 1 - core, m], pair_r.at[self.a, m], *self.sems(m), core_dev)

        def pair_wait(self, m):
            arrived(pair_r.at[self.a, m], self.sems(m)[1], core_dev)

        def q(self, m, zz):
            return part[core, m, zz] + pair_r[self.a, m, zz].astype(F32)

        def step(self, s):
            a = self.a
            for way in (0, 1):
                off = half + 1 - s
                zz = zmod(z + off) if way == 0 else zmod(z - off)
                k = 2 + way * half + (s - 1)
                if s > 1:
                    pk = 2 + way * half + (s - 2)
                    if s == 2:
                        arrived(ring_r.at[a, way, 0, way], self.sems(pk)[1], z_dev[1 - way])
                    else:
                        arrived(ring_r.at[a, way, s - 2], self.sems(pk)[1], z_dev[1 - way])
                for m in (0, 1):
                    if s == 1 and m != way:
                        continue
                    val = self.q(m, zz)
                    if s > 2 or (s == 2 and m == way):
                        val += ring_r[a, way, s - 2, m].astype(F32)
                    ring_s[a, way, s - 1, m] = val.astype(BF16)
                if s == 1:
                    send(ring_s.at[a, way, 0, way], ring_r.at[a, way, 0, way], *self.sems(k), z_dev[way])
                else:
                    send(ring_s.at[a, way, s - 1], ring_r.at[a, way, s - 1], *self.sems(k), z_dev[way])

        def last(self):
            a = self.a
            for way in (0, 1):
                k = 2 + way * half + half - 1
                arrived(ring_r.at[a, way, half - 1], self.sems(k)[1], z_dev[1 - way])
            for m in (0, 1):
                val = self.q(m, z)
                val += ring_r[a, 0, half - 1, m].astype(F32)
                val += ring_r[a, 1, half - 1, m].astype(F32)
                fin[m] = val
                fin_s[a, m] = val.astype(BF16)
            send(fin_s.at[a, 1 - x], fin_r.at[a], *self.sems(2 + 2 * half), x_dev)

        def result(self, o):
            mine = fin[x]
            arrived(fin_r.at[self.a], self.sems(2 + 2 * half)[1], x_dev)
            o[...] = (mine + fin_r[self.a].astype(F32)).astype(BF16)

    def flat(ref, m):
        per_m = chunk // blk
        return ref[m * per_m : (m + 1) * per_m].reshape(chunk, hidden)

    def example(ref, e):
        n = SEQ // blk
        return ref[e * n : (e + 1) * n].reshape(SEQ, hidden)

    def norm_down(e):
        cote = cotp[e * SEQ : (e + 1) * SEQ]
        he = example(hid, e)
        acc = jnp.zeros((1, width), F32)
        for j in range(nbh):
            gg = dot(he[:, j * BLK : (j + 1) * BLK], cote, 0, 0)
            acc += jnp.sum(gg * gg, axis=0, keepdims=True) * md[j : j + 1, :]
        return jnp.sum(acc)

    def norm_up(e):
        toke = tokp[e * SEQ : (e + 1) * SEQ]
        pge = example(pg, e)
        acc = jnp.zeros((1, hidden), F32)
        for i in range(nbu):
            gg = dot(toke[:, i * BLK : (i + 1) * BLK], pge, 0, 0)
            acc += jnp.sum(gg * gg, axis=0, keepdims=True) * mu[i : i + 1, :]
        return jnp.sum(acc)

    ro = RowSum(0)
    gather_wait(2, hid)
    for m in range(2):
        ro.rows_of(m, dot(flat(hid, m), dnm[...], 1, 0))
    ro.pair_wait(0)
    ro.pair_wait(1)
    down_sq = []
    for s in range(1, half + 1):
        ro.step(s)
        if s <= EX:
            down_sq.append(norm_down(s - 1))
    ro.last()
    ro.result(out_o)

    ri = RowSum(1)
    gather_wait(3, pg)
    for m in range(2):
        ri.rows_of(m, dot(flat(pg, m), upm[...], 1, 1))
    up_sq = [norm_up(0)]
    ri.pair_wait(0)
    ri.pair_wait(1)
    ri.step(1)
    up_sq += [norm_up(1), norm_up(2)]
    ri.step(2)
    up_sq += [norm_up(3)]

    groups = [
        [(c_at(k), c_at(nc - k)) for k in range(1, nc)],
        [(z_at(k), z_at(nz - k)) for k in range(1, nz)],
        [(core_dev, core_dev), (x_dev, x_dev), (xc_dev, xc_dev)],
    ]

    def sq_send(g):
        sq_s[g] = sq_a[...]
        for k, (dev, _) in enumerate(groups[g]):
            send(sq_s.at[g], sq_r.at[g, k], sq_ss.at[g, k], sq_rs.at[g, k], dev)

    def sq_sum(g):
        total = sq_a[...]
        for k, (_, dev) in enumerate(groups[g]):
            arrived(sq_r.at[g, k], sq_rs.at[g, k], dev)
            total += sq_r[g, k]
        sq_a[...] = total

    sq_a[...] = jnp.zeros_like(sq_a)
    for e in range(EX):
        sq_a[e : e + 1, :] = jnp.full((1, BLK), up_sq[e] + down_sq[e])
    sq_send(0)
    ri.step(3)
    sq_sum(0)
    sq_send(1)
    ri.step(4)
    sq_sum(1)
    sq_send(2)
    ri.last()
    sq_sum(2)

    for e in range(EX):
        total = sq_a[e : e + 1, :]
        bound = clip[e].astype(F32) * BOUND
        f = jnp.minimum(1.0, bound / jnp.sqrt(total + 1e-6))[:, 0:1]
        n = SEQ // blk
        psc[e * SEQ : (e + 1) * SEQ] = (example(pg, e).astype(F32) * f).astype(BF16)
        at = slice(e * SEQ, (e + 1) * SEQ)
        csc[at] = (cotp[at].astype(F32) * f).astype(BF16)

    hf = hid[...].reshape(tokens, hidden)
    tile = 256
    outs = []
    for i in range(width // tile):
        at = slice(i * tile, (i + 1) * tile)
        g2 = dot(tokp[:, at], psc[...], 0, 0)
        for h in range(tile // BLK):
            lo = i * tile + h * BLK
            row = mu[lo // BLK : lo // BLK + 1, :] * UNIT
            uo[lo : lo + BLK, :] = (g2[h * BLK : (h + 1) * BLK] * row).astype(BF16)
        cp = pltpu.make_async_copy(uo.at[at], up_o.at[at], loc_sem.at[4 + i])
        cp.start()
        outs.append(cp)
    for i in range(hidden // tile):
        at = slice(i * tile, (i + 1) * tile)
        g2 = dot(hf[:, at], csc[...], 0, 0)
        for h in range(tile // BLK):
            lo = i * tile + h * BLK
            row = md[lo // BLK : lo // BLK + 1, :] * UNIT
            do[lo : lo + BLK, :] = (g2[h * BLK : (h + 1) * BLK] * row).astype(BF16)
        cp = pltpu.make_async_copy(do.at[at], dn_o.at[at], loc_sem.at[4 + width // tile + i])
        cp.start()
        outs.append(cp)
    ri.result(ing_o)
    for cp in outs:
        cp.wait()
    for copy in pending:
        copy.wait_send()


def solution(mesh):
    nz = mesh.shape["row"] // 4
    nc = mesh.shape["col"]

    def local(tok, cot, up, dn, upk, dnk, clip):
        width, hidden = up.shape
        tokens = tok.shape[0] * mesh.shape["row"]
        blk = tokens // nc
        half = nz // 2
        any_, vm, sm = (pl.BlockSpec(memory_space=m) for m in (pl.ANY, pltpu.VMEM, pltpu.SMEM))
        dma = pltpu.SemaphoreType.DMA
        n_ag = 1 + 4 * half + 2 * nz
        n_row = 3 + 2 * half
        return pl.pallas_call(
            functools.partial(kernel, nz, nc),
            out_shape=(
                jax.ShapeDtypeStruct(tok.shape, BF16),
                jax.ShapeDtypeStruct(tok.shape, BF16),
                jax.ShapeDtypeStruct(up.shape, BF16),
                jax.ShapeDtypeStruct(dn.shape, BF16),
            ),
            in_specs=[vm, vm, any_, any_, sm, sm, sm],
            out_specs=(vm, vm, any_, any_),
            scratch_shapes=[
                pltpu.VMEM((tokens, width), BF16),
                pltpu.VMEM((tokens, width), BF16),
                pltpu.VMEM((width, hidden), BF16),
                pltpu.VMEM((hidden, width), BF16),
                pltpu.VMEM((16, hidden), F32),
                pltpu.VMEM((8, width), F32),
                pltpu.VMEM((2, nc, blk, hidden), BF16),
                pltpu.VMEM((2, nc, blk, hidden), BF16),
                pltpu.VMEM((nc, blk, hidden), BF16),
                pltpu.VMEM((nc, blk, hidden), BF16),
                pltpu.VMEM((blk, hidden), F32),
                pltpu.VMEM((2, 2, nz, SUB, width), F32),
                pltpu.VMEM((2, 2, 2, nz, SUB, width), BF16),
                pltpu.VMEM((2, 2, nz, SUB, width), BF16),
                pltpu.VMEM((2, 2, half, 2, SUB, width), BF16),
                pltpu.VMEM((2, 2, half, 2, SUB, width), BF16),
                pltpu.VMEM((2, SUB, width), F32),
                pltpu.VMEM((2, 2, SUB, width), BF16),
                pltpu.VMEM((2, SUB, width), BF16),
                pltpu.VMEM((8, BLK), F32),
                pltpu.VMEM((3, 8, BLK), F32),
                pltpu.VMEM((3, 8, 8, BLK), F32),
                pltpu.VMEM((tokens, hidden), BF16),
                pltpu.VMEM((tokens, width), BF16),
                pltpu.VMEM((width, hidden), BF16),
                pltpu.VMEM((hidden, width), BF16),
                dma((16,)),
                dma((2, n_ag)),
                dma((2, n_ag)),
                dma((4, nc)),
                dma((4, nc)),
                dma((2, n_row)),
                dma((2, n_row)),
                dma((3, 8)),
                dma((3, 8)),
            ],
            compiler_params=pltpu.CompilerParams(
                collective_id=0, has_side_effects=True, vmem_limit_bytes=56 * 1024 * 1024
            ),
        )(tok, cot, up, dn, upk, dnk, clip)

    placed = (
        P("row", "col"),
        P("row", "col"),
        P("col", "row"),
        P("row", "col"),
        P("col", "row"),
        P("row", "col"),
        P(),
    )
    return jax.shard_map(
        local,
        mesh=mesh,
        in_specs=placed,
        out_specs=(P("row", "col"), P("row", "col"), P("col", "row"), P("row", "col")),
        check_vma=False,
    )
```

time: 598 us -> 126 us (0.21)
  waiting for transfers between devices: 364 us -> 0 us
  blocking collectives: 150 us -> 0 us
  Pallas kernels: 0 us -> 116 us
  matrix products: 35.9 us -> 0 us
  between operations: 14.2 us -> 0.64 us
  local copies, waits for them, and re-layouts: 19.3 us -> 8.99 us
  other arithmetic: 10.3 us -> 0 us
    reduce_scatter x4 -> x0, waiting for transfers between devices: 237 us -> none  [the longest x1 84.3 us: local(): lax.psum_scatter(jnp.dot(block_rows, down_tile, preferred_element_type=jn...]
    all_gather x2 -> x0, waiting for transfers between devices: 125 us -> none  [the longest x1 64.7 us: local(): token_panel = lax.all_gather(tokens, 'row', axis=0, tiled=True)]
    pallas_call x0 -> x1, Pallas kernels: none -> 116 us  [local(): pl.pallas_call(functools.partial(kernel, nz, nc), out_shape=(jax.ShapeDty...]
    psum x1 -> x0, blocking collectives: 85.5 us -> none  [local(): squared = lax.psum(local_squares, ('row', 'col'))]
    all_gather x2 -> x0, blocking collectives: 64.5 us -> none  [the longest x1 32.3 us: local(): lax.all_gather(act_part.astype(jnp.bfloat16), 'col', axis=0, tiled=True)]
    dot_general x8 -> x0, matrix products: 35.9 us -> none  [the longest x1 5.34 us: local(): lax.dot_general(token_panel, pre_scaled, (((0,), (0,)), ((), ())), prefer...]
    convert_element_type x7 -> x0, other arithmetic: 7.77 us -> none  [the longest x1 2.29 us: local(): up_each = up_each * up_mask[None]]
    unnamed x23 -> x7, local copies, waits for them, and re-layouts: 13.9 us -> 8.99 us
  transfers between devices with their start and end apart: 6 -> 0, of which waited for: 5 -> 0; matrix products, arithmetic and copies ran while one was open for 9% -> 0% of each run, Pallas kernels for 0% -> 0%
where the time goes in v1:
time: 126 us; the launch traced here: 125 us
  Pallas kernels  116 us (92%)
  local copies, waits for them, and re-layouts  8.99 us (7%)
    pallas_call x1, Pallas kernels, local(): pl.pallas_call(functools.partial(kernel, nz, nc), out_shape=(jax.ShapeDty...  116 us
    unnamed x7, local copies, waits for them, and re-layouts  8.99 us

profile of v1, /device:TPU:1, one launch (start us, length us, event | category | flops | bytes accessed | tf_op | source)
XLA Modules:
  0.0 125.5 jit_solution(7633227908396050581)
XLA Ops:
  0.6 1.4 %copy.11.upk = s32[12,6]{1,0:T(8,128)} copy(s32[12,6]{0,1:T(8,128)} %param.11) | data formatting | bytes 576 | tf_op args[4]
  2.0 115.9 %shard_map.102 = (bf16[16,1536]{1,0:T(8,128)(2,1)}, bf16[16,1536]{1,0:T(8,128)(2,1)}, bf16[1536,768]{1,0:T(8,128)(2,1)}, bf16[768,1536]{1,0:T(8,128)(2,1)}) custom-call(bf16[16,1536]{1,0:T(8,128)(2,1)} %tok.1, bf16[16,1536]{1,0:T(8,128)(2,1)} %cot.1, bf16[1536,768]{1,0:T(8,128)(2,1)} %up.1, bf16[768,1536]{1,0:T(8,128)(2,1)} %dn.1, s32[12,6]{1,0:T(8,128)} %copy.11.upk, ...), custom_call_target="tpu_custom_call" | custom-call | tf_op jit(solution)/shard_map/pallas_call | solution.py:450
  117.9 1.4 %copy.16 = bf16[16,1536]{1,0:T(8,128)(2,1)} copy(bf16[16,1536]{1,0:T(8,128)(2,1)} %get-tuple-element.8) | data formatting | bytes 98304
  119.3 1.4 %copy.17 = bf16[16,1536]{1,0:T(8,128)(2,1)} copy(bf16[16,1536]{1,0:T(8,128)(2,1)} %get-tuple-element.9) | data formatting | bytes 98304
  120.7 0.0 copy-start
  120.7 3.4 %copy.18 = bf16[1536,768]{1,0:T(8,128)(2,1)} copy(bf16[1536,768]{1,0:T(8,128)(2,1)} %get-tuple-element.10) | data formatting | bytes 4718592
  124.1 0.0 copy-done
  124.1 1.4 %copy.19 = bf16[768,1536]{1,0:T(8,128)(2,1)} copy(bf16[768,1536]{1,0:T(8,128)(2,1)S(1)} %copy-done) | data formatting | bytes 4718592
Async XLA Ops:
  120.7 3.4 %copy-start = (bf16[768,1536]{1,0:T(8,128)(2,1)S(1)}, bf16[768,1536]{1,0:T(8,128)(2,1)}, u32[]{:S(2)}) copy-start(bf16[768,1536]{1,0:T(8,128)(2,1)} %get-tuple-element.11) | copy-start | bytes 7077892

commit v2 on v1

v2 whole, which is shorter than its diff:
```python
import functools
import math

import jax
import jax.numpy as jnp
from jax import lax
from jax.experimental import pallas as pl
from jax.experimental.pallas import tpu as pltpu
from jax.sharding import PartitionSpec as P

MESH = pl.DeviceIdType.MESH
D = 12288
FF = 24576
SEQ = 128
BLK = 128
EX = 4
SUB = 16
F32 = jnp.float32
BF16 = jnp.bfloat16
ROOT = math.sqrt(2.0 / math.pi)
ROW_KEYS = [("x", 4), ("x", 3), ("x", -3), ("x", 2), ("x", -2), ("x", 0), ("n", 1), ("n", -1)]
ROW_KEYS += [("r", 4), ("r", 3), ("r", -3), ("z", 2), ("z", -2)]
UNIT = 7.0 / (EX * math.sqrt(SEQ))
BOUND = math.sqrt(D * FF * SEQ) / 1000.0


def dot(a, b, ca, cb):
    return lax.dot_general(a, b, (((ca,), (cb,)), ((), ())), preferred_element_type=F32)


def kernel(
    nz, nc,
    tok, cot, up, dn, upk, dnk, clip,
    out_o, ing_o, up_o, dn_o,
    tokp, cotp, upm, dnm, mu, md,
    send_h, recv_h, hid, pg, dact,
    part, pair, pair_r, row_out, row_in, near_out, near_in, fin, res,
    sq_a, sq_s, sq_r, psc, csc, uo, do,
    loc_sem, ag_s, ag_r, col_s, col_r, row_s, row_r, sq_ss, sq_rs,
):
    tokens = tok.shape[0] * 4 * nz
    width = tok.shape[1]
    hidden = up.shape[1]
    r = lax.axis_index("row")
    c = lax.axis_index("col")
    core = lax.rem(r, 2)
    z = lax.rem(lax.div(r, 2), nz)
    x = lax.div(r, 2 * nz)

    def row_of(xx, zz, kk):
        return (xx * nz + zz) * 2 + kk

    def zmod(v):
        return lax.rem(v + 2 * nz, nz)

    core_dev = (row_of(x, z, 1 - core), c)
    x_dev = (row_of(1 - x, z, core), c)

    def z_at(k):
        return (row_of(x, zmod(z + k), core), c)

    def c_at(k):
        return (r, lax.rem(c + k, nc))

    up_in = pltpu.make_async_copy(up, upm, loc_sem.at[0])
    dn_in = pltpu.make_async_copy(dn, dnm, loc_sem.at[1])
    up_in.start()
    dn_in.start()

    def rows(ref, xx, zz, kk):
        return ref.at[pl.ds(pl.multiple_of(row_of(xx, zz, kk) * SUB, SUB), SUB)]

    own = [
        pltpu.make_async_copy(tok, rows(tokp, x, z, core), loc_sem.at[2]),
        pltpu.make_async_copy(cot, rows(cotp, x, z, core), loc_sem.at[3]),
    ]
    own[0].start()
    own[1].start()

    barrier = pltpu.get_barrier_semaphore()
    near_c = [(0, 1)] + [(k, kk) for k in range(1, nc) for kk in (0, 1)]
    near_z = [(0, 1)] + [(k, m) for k in range(1, nz) for m in (0, 1)]

    def cc_at(k, kk):
        return (row_of(x, z, core if kk == 0 else 1 - core), lax.rem(c + k, nc))

    def xz_at(k, m):
        return (row_of(x if m == 0 else 1 - x, zmod(z + k), core), c)

    peers = [cc_at(*p) for p in near_c] + [xz_at(*p) for p in near_z]
    for dev in peers:
        pl.semaphore_signal(barrier, inc=1, device_id=dev, device_id_type=MESH)
    pl.semaphore_wait(barrier, len(peers))
    own[0].wait()
    own[1].wait()

    pending = []

    def send(src, dst, ssem, rsem, dev):
        copy = pltpu.make_async_remote_copy(
            src_ref=src, dst_ref=dst, send_sem=ssem, recv_sem=rsem, device_id=dev, device_id_type=MESH
        )
        copy.start()
        pending.append(copy)
        return copy

    def arrived(dst, rsem, dev):
        pltpu.make_async_remote_copy(
            src_ref=dst, dst_ref=dst, send_sem=rsem, recv_sem=rsem, device_id=dev, device_id_type=MESH
        ).wait_recv()

    class Gather:
        def __init__(self, a, shard, panel):
            self.a, self.shard, self.panel, self.keys = a, shard, panel, {}

        def sems(self, key):
            k = self.keys.setdefault(key, len(self.keys))
            return ag_s.at[self.a, k], ag_r.at[self.a, k]

        def slot(self, stream, off, kk=None):
            xx = x if stream == 0 else 1 - x
            return rows(self.panel, xx, zmod(z + off), core if kk is None else kk)

        def put(self, stream, off, key, dev):
            ref = self.slot(stream, off)
            send(ref, ref, *self.sems(key), dev)

        def take(self, stream, off, key):
            arrived(self.slot(stream, off), self.sems(key)[1], x_dev)

        def core_put(self, stream, off):
            self.put(stream, off, ("core", stream, off % nz), core_dev)

        def x_put(self, off):
            self.put(0, off, ("x", off % nz), x_dev)

        def start(self):
            for way, sign in ((0, 1), (1, -1)):
                self.put(0, 0, ("z", 0, sign), z_at(sign))
                self.put(0, 0, ("z", 0, 2 * sign), z_at(2 * sign))
            self.x_put(0)
            self.core_put(0, 0)

        def partner(self):
            self.take(1, 0, ("x", 0))
            for sign in (1, -1):
                self.put(1, 0, ("z", 1, sign), z_at(sign))
            self.core_put(1, 0)

        def near(self):
            for sign in (1, -1):
                self.take(0, -2 * sign, ("z", 0, 2 * sign))
                self.put(0, -2 * sign, ("z", 0, 3 * sign), z_at(sign))
                if sign == (1, -1)[self.a]:
                    self.put(0, -2 * sign, ("z", 0, 4), z_at(2 * sign))
                self.x_put(-2 * sign)
                self.core_put(0, -2 * sign)
            for sign in (1, -1):
                self.take(0, -sign, ("z", 0, sign))
                self.core_put(0, -sign)

        def far(self):
            for sign in (1, -1):
                self.take(0, -3 * sign, ("z", 0, 3 * sign))
                self.x_put(-3 * sign)
                self.core_put(0, -3 * sign)
            self.take(0, 4, ("z", 0, 4))
            self.x_put(4)
            self.core_put(0, 4)
            for sign in (1, -1):
                self.take(1, -sign, ("z", 1, sign))
                self.core_put(1, -sign)

        def finish(self):
            for off in (2, -2, 3, -3, 4):
                self.take(1, off, ("x", off % nz))
                self.core_put(1, off)
            for stream in (0, 1):
                for off in range(nz):
                    key = ("core", stream, off)
                    arrived(self.slot(stream, off, 1 - core), self.sems(key)[1], core_dev)

    gt = Gather(0, tok, tokp)
    gc = Gather(1, cot, cotp)
    gt.start()
    gt.partner()
    gt.near()
    gc.start()

    nbu, nbh = width // BLK, hidden // BLK
    for i in range(nbu):
        for j in range(nbh):
            mu[i : i + 1, j * BLK : (j + 1) * BLK] = jnp.full((1, BLK), upk[j, i].astype(F32))
            md[j : j + 1, i * BLK : (i + 1) * BLK] = jnp.full((1, BLK), dnk[j, i].astype(F32))
    up_in.wait()

    @pl.loop(0, nbu)
    def _(i):
        at = pl.ds(pl.multiple_of(i * BLK, BLK), BLK)
        upm[at, :] = upm[at, :] * mu[pl.ds(i, 1), :].astype(BF16)

    gt.far()
    gc.partner()
    dn_in.wait()

    @pl.loop(0, nbh)
    def _(j):
        at = pl.ds(pl.multiple_of(j * BLK, BLK), BLK)
        dnm[at, :] = dnm[at, :] * md[pl.ds(j, 1), :].astype(BF16)

    gc.near()
    gt.finish()

    blk = tokens // nc
    chunk = 256
    per = chunk // blk
    n_chunk = tokens // chunk

    def col_send(a, src, dst, q, k):
        return send(src, dst, col_s.at[a, k], col_r.at[a, k], (r, q))

    def scatter_chunk(a, m, value):
        for b in range(per):
            send_h[a, m * per + b] = value[b * blk : (b + 1) * blk].astype(BF16)

    def scatter_send(a):
        for k in range(1, nc):
            q = lax.rem(c + k, nc)
            col_send(a, send_h.at[a, q], recv_h.at[a, k], q, k)

    def scatter_sum(a):
        total = send_h[a, c].astype(F32)
        for k in range(1, nc):
            arrived(recv_h.at[a, k], col_r.at[a, k], c_at(nc - k))
            total += recv_h[a, k].astype(F32)
        return total

    def gather_send(a, panel):
        for k in range(1, nc):
            col_send(a, panel.at[c], panel.at[c], lax.rem(c + k, nc), k)

    def gather_wait(a, panel):
        for k in range(1, nc):
            q = lax.rem(c + nc - k, nc)
            arrived(panel.at[q], col_r.at[a, k], (r, q))

    for m in range(n_chunk):
        scatter_chunk(0, m, dot(tokp[m * chunk : (m + 1) * chunk], upm[...], 1, 0))
    scatter_send(0)

    gc.far()
    gc.finish()

    for m in range(n_chunk):
        scatter_chunk(1, m, dot(cotp[m * chunk : (m + 1) * chunk], dnm[...], 1, 1))
    scatter_send(1)

    v = scatter_sum(0)
    t = jnp.tanh(ROOT * (v + 0.044715 * (v * v * v)))
    hid[c] = (0.5 * v * (1.0 + t)).astype(BF16)
    gather_send(2, hid)
    dact[...] = 0.5 * (1.0 + t) + (0.5 * ROOT) * v * (1.0 - t * t) * (1.0 + 0.134145 * (v * v))

    g = scatter_sum(1)
    pg[c] = (g * dact[...]).astype(BF16)
    gather_send(3, pg)

    outs = []

    class RowSum:
        def __init__(self, a):
            self.a = a

        def sems(self, k):
            return row_s.at[self.a, k], row_r.at[self.a, k]

        def rows_of(self, m, value):
            v4 = value.reshape(nz, 2, SUB, width)
            part[self.a, 0, m] = v4[:, 0]
            part[self.a, 1, m] = v4[:, 1]
            pair[self.a, 0, m] = v4[:, 0].astype(BF16)
            pair[self.a, 1, m] = v4[:, 1].astype(BF16)
            send(pair.at[self.a, 1 - core, m], pair_r.at[self.a, m], *self.sems(m), core_dev)

        def pair_wait(self, m):
            arrived(pair_r.at[self.a, m], self.sems(m)[1], core_dev)

        def q(self, m, zz):
            return part[self.a, core, m, zz] + pair_r[self.a, m, zz].astype(F32)

        def key(self, name):
            return self.sems(2 + ROW_KEYS.index(name))

        def out(self, slot, name, dev):
            send(row_out.at[self.a, slot], row_in.at[self.a, slot], *self.key(name), dev)

        def get(self, slot, name):
            arrived(row_in.at[self.a, slot], self.key(name)[1], x_dev)

        def along_x(self):
            for slot, off in enumerate((4, 3, -3, 2, -2)):
                row_out[self.a, slot] = self.q(1 - x, zmod(z + off)).astype(BF16)
                self.out(slot, ("x", off), x_dev)
            for way, sign in ((0, 1), (1, -1)):
                for m in (0, 1):
                    near_out[self.a, way, m] = self.q(m, zmod(z + sign)).astype(BF16)
                send(near_out.at[self.a, way], near_in.at[self.a, way], *self.key(("n", sign)), z_at(sign))

        def relay(self):
            sign = (1, -1)[self.a]
            for slot, off, hop in ((0, 4, 2 * sign), (1, 3, 1), (2, -3, -1)):
                self.get(slot, ("x", off))
                val = self.q(x, zmod(z + off)) + row_in[self.a, slot].astype(F32)
                row_out[self.a, 5 + slot] = val.astype(BF16)
                self.out(5 + slot, ("r", off), z_at(hop))

        def near(self):
            for way, sign in ((0, 1), (1, -1)):
                arrived(near_in.at[self.a, way], self.key(("n", sign))[1], x_dev)
            for m in (0, 1):
                val = self.q(m, z)
                for way in (0, 1):
                    val += near_in[self.a, way, m].astype(F32)
                fin[self.a, m] = val
            row_out[self.a, 10] = fin[self.a, 1 - x].astype(BF16)
            self.out(10, ("x", 0), x_dev)

        def along_z(self):
            for way, sign in ((0, 1), (1, -1)):
                self.get(3 + way, ("x", 2 * sign))
                self.get(6 + way, ("r", 3 * sign))
                val = self.q(x, zmod(z + 2 * sign)) + row_in[self.a, 3 + way].astype(F32)
                val += row_in[self.a, 6 + way].astype(F32)
                if way == self.a:
                    self.get(5, ("r", 4))
                    val += row_in[self.a, 5].astype(F32)
                row_out[self.a, 8 + way] = val.astype(BF16)
                self.out(8 + way, ("z", 2 * sign), z_at(2 * sign))

        def result(self, o, sem):
            self.get(10, ("x", 0))
            val = fin[self.a, x] + row_in[self.a, 10].astype(F32)
            for way, sign in ((0, 1), (1, -1)):
                self.get(8 + way, ("z", 2 * sign))
                val += row_in[self.a, 8 + way].astype(F32)
            res[self.a] = val.astype(BF16)
            cp = pltpu.make_async_copy(res.at[self.a], o, sem)
            cp.start()
            outs.append(cp)

    def flat(ref, m):
        per_m = chunk // blk
        return ref[m * per_m : (m + 1) * per_m].reshape(chunk, hidden)

    def example(ref, e):
        n = SEQ // blk
        return ref[e * n : (e + 1) * n].reshape(SEQ, hidden)

    def norm_down(e):
        cote = cotp[e * SEQ : (e + 1) * SEQ]
        he = example(hid, e)
        acc = jnp.zeros((1, width), F32)
        for j in range(nbh):
            gg = dot(he[:, j * BLK : (j + 1) * BLK], cote, 0, 0)
            acc += jnp.sum(gg * gg, axis=0, keepdims=True) * md[j : j + 1, :]
        return jnp.sum(acc)

    def norm_up(e):
        toke = tokp[e * SEQ : (e + 1) * SEQ]
        pge = example(pg, e)
        acc = jnp.zeros((1, hidden), F32)
        for i in range(nbu):
            gg = dot(toke[:, i * BLK : (i + 1) * BLK], pge, 0, 0)
            acc += jnp.sum(gg * gg, axis=0, keepdims=True) * mu[i : i + 1, :]
        return jnp.sum(acc)

    groups = [
        [(cc_at(k, kk), cc_at(nc - k, kk)) for k, kk in near_c],
        [(xz_at(k, m), xz_at(nz - k, m)) for k, m in near_z],
    ]

    def sq_send(g):
        sq_s[g] = sq_a[...]
        for k, (dev, _) in enumerate(groups[g]):
            send(sq_s.at[g], sq_r.at[g, k], sq_ss.at[g, k], sq_rs.at[g, k], dev)

    def sq_sum(g):
        total = sq_a[...]
        for k, (_, dev) in enumerate(groups[g]):
            arrived(sq_r.at[g, k], sq_rs.at[g, k], dev)
            total += sq_r[g, k]
        sq_a[...] = total

    tile = 256

    def scale():
        for e in range(EX):
            total = sq_a[e : e + 1, :]
            bound = clip[e].astype(F32) * BOUND
            f = jnp.minimum(1.0, bound / jnp.sqrt(total + 1e-6))[:, 0:1]
            psc[e * SEQ : (e + 1) * SEQ] = (example(pg, e).astype(F32) * f).astype(BF16)
            at = slice(e * SEQ, (e + 1) * SEQ)
            csc[at] = (cotp[at].astype(F32) * f).astype(BF16)

    def update_up():
        for i in range(width // tile):
            at = slice(i * tile, (i + 1) * tile)
            g2 = dot(tokp[:, at], psc[...], 0, 0)
            for h in range(tile // BLK):
                lo = i * tile + h * BLK
                row = mu[lo // BLK : lo // BLK + 1, :] * UNIT
                uo[lo : lo + BLK, :] = (g2[h * BLK : (h + 1) * BLK] * row).astype(BF16)
            cp = pltpu.make_async_copy(uo.at[at], up_o.at[at], loc_sem.at[6 + i])
            cp.start()
            outs.append(cp)

    def update_down():
        hf = hid[...].reshape(tokens, hidden)
        for i in range(hidden // tile):
            at = slice(i * tile, (i + 1) * tile)
            g2 = dot(hf[:, at], csc[...], 0, 0)
            for h in range(tile // BLK):
                lo = i * tile + h * BLK
                row = md[lo // BLK : lo // BLK + 1, :] * UNIT
                do[lo : lo + BLK, :] = (g2[h * BLK : (h + 1) * BLK] * row).astype(BF16)
            cp = pltpu.make_async_copy(do.at[at], dn_o.at[at], loc_sem.at[6 + width // tile + i])
            cp.start()
            outs.append(cp)

    ro, ri = RowSum(0), RowSum(1)
    gather_wait(2, hid)
    for m in range(2):
        ro.rows_of(m, dot(flat(hid, m), dnm[...], 1, 0))
    down_sq = [norm_down(e) for e in range(EX)]
    ro.pair_wait(0)
    ro.pair_wait(1)
    ro.along_x()
    ro.relay()
    ro.near()

    gather_wait(3, pg)
    for m in range(2):
        ri.rows_of(m, dot(flat(pg, m), upm[...], 1, 1))
    sq_a[...] = jnp.zeros_like(sq_a)
    for e in range(EX):
        sq_a[e : e + 1, :] = jnp.full((1, BLK), norm_up(e) + down_sq[e])
    sq_send(0)
    ro.along_z()
    ri.pair_wait(0)
    ri.pair_wait(1)
    ri.along_x()
    ri.relay()
    sq_sum(0)
    sq_send(1)
    ro.result(out_o, loc_sem.at[4])
    ri.near()
    ri.along_z()
    sq_sum(1)
    scale()
    update_up()
    update_down()
    ri.result(ing_o, loc_sem.at[5])
    for cp in outs:
        cp.wait()
    for copy in pending:
        copy.wait_send()


def settle(*refs):
    sem = refs[-1]
    copies = []
    for i in range(4):
        src, dst = refs[i], refs[4 + i]
        pieces = 1 if src.shape[0] < 64 else 6
        step = src.shape[0] // pieces
        for p in range(pieces):
            at = pl.ds(p * step, step)
            copies.append(pltpu.make_async_copy(src.at[at], dst.at[at], sem.at[len(copies)]))
    for cp in copies:
        cp.start()
    for cp in copies:
        cp.wait()


def solution(mesh):
    nz = mesh.shape["row"] // 4
    nc = mesh.shape["col"]

    def local(tok, cot, up, dn, upk, dnk, clip):
        width, hidden = up.shape
        tokens = tok.shape[0] * mesh.shape["row"]
        blk = tokens // nc
        any_, vm, sm = (pl.BlockSpec(memory_space=m) for m in (pl.ANY, pltpu.VMEM, pltpu.SMEM))
        dma = pltpu.SemaphoreType.DMA
        n_ag = 32
        n_row = 2 + len(ROW_KEYS)
        shapes = (
            jax.ShapeDtypeStruct(tok.shape, BF16),
            jax.ShapeDtypeStruct(tok.shape, BF16),
            jax.ShapeDtypeStruct(up.shape, BF16),
            jax.ShapeDtypeStruct(dn.shape, BF16),
        )
        made = pl.pallas_call(
            functools.partial(kernel, nz, nc),
            out_shape=shapes,
            in_specs=[any_] * 4 + [sm] * 3,
            out_specs=(any_,) * 4,
            scratch_shapes=[
                pltpu.VMEM((tokens, width), BF16),
                pltpu.VMEM((tokens, width), BF16),
                pltpu.VMEM((width, hidden), BF16),
                pltpu.VMEM((hidden, width), BF16),
                pltpu.VMEM((16, hidden), F32),
                pltpu.VMEM((8, width), F32),
                pltpu.VMEM((2, nc, blk, hidden), BF16),
                pltpu.VMEM((2, nc, blk, hidden), BF16),
                pltpu.VMEM((nc, blk, hidden), BF16),
                pltpu.VMEM((nc, blk, hidden), BF16),
                pltpu.VMEM((blk, hidden), F32),
                pltpu.VMEM((2, 2, 2, nz, SUB, width), F32),
                pltpu.VMEM((2, 2, 2, nz, SUB, width), BF16),
                pltpu.VMEM((2, 2, nz, SUB, width), BF16),
                pltpu.VMEM((2, 11, SUB, width), BF16),
                pltpu.VMEM((2, 11, SUB, width), BF16),
                pltpu.VMEM((2, 2, 2, SUB, width), BF16),
                pltpu.VMEM((2, 2, 2, SUB, width), BF16),
                pltpu.VMEM((2, 2, SUB, width), F32),
                pltpu.VMEM((2, SUB, width), BF16),
                pltpu.VMEM((8, BLK), F32),
                pltpu.VMEM((2, 8, BLK), F32),
                pltpu.VMEM((2, 16, 8, BLK), F32),
                pltpu.VMEM((tokens, hidden), BF16),
                pltpu.VMEM((tokens, width), BF16),
                pltpu.VMEM((width, hidden), BF16),
                pltpu.VMEM((hidden, width), BF16),
                dma((24,)),
                dma((2, n_ag)),
                dma((2, n_ag)),
                dma((4, nc)),
                dma((4, nc)),
                dma((2, n_row)),
                dma((2, n_row)),
                dma((2, 16)),
                dma((2, 16)),
            ],
            compiler_params=pltpu.CompilerParams(
                collective_id=0, has_side_effects=True, vmem_limit_bytes=56 * 1024 * 1024
            ),
        )(tok, cot, up, dn, upk.T, dnk, clip)
        return pl.pallas_call(
            settle,
            out_shape=shapes,
            in_specs=[any_] * 4,
            out_specs=(any_,) * 4,
            scratch_shapes=[dma((16,))],
            compiler_params=pltpu.CompilerParams(vmem_limit_bytes=60 * 1024 * 1024),
        )(*made)

    placed = (
        P("row", "col"),
        P("row", "col"),
        P("col", "row"),
        P("row", "col"),
        P("col", "row"),
        P("row", "col"),
        P(),
    )
    return jax.shard_map(
        local,
        mesh=mesh,
        in_specs=placed,
        out_specs=(P("row", "col"), P("row", "col"), P("col", "row"), P("row", "col")),
        check_vma=False,
    )
```

time: 126 us -> 247 us (1.96)
  Pallas kernels: 116 us -> 245 us
  local copies, waits for them, and re-layouts: 8.99 us -> 0 us
    pallas_call x1 -> x2, Pallas kernels: 116 us -> 245 us  [the longest x1 147 us: local(): pl.pallas_call(settle, out_shape=shapes, in_specs=[any_] * 4, out_specs=(...]
    unnamed x7 -> x0, local copies, waits for them, and re-layouts: 8.99 us -> none
where the time goes in v2:
time: 247 us; the launch traced here: 246 us
  Pallas kernels  245 us (99%)
    pallas_call x1, Pallas kernels, local(): pl.pallas_call(settle, out_shape=shapes, in_specs=[any_] * 4, out_specs=(...  147 us
    pallas_call x1, Pallas kernels, local(): pl.pallas_call(functools.partial(kernel, nz, nc), out_shape=shapes, in_sp...  97.8 us

profile of v2, /device:TPU:1, one launch (start us, length us, event | category | flops | bytes accessed | tf_op | source)
XLA Modules:
  0.0 245.6 jit_solution(9819636176463155192)
XLA Ops:
  0.6 97.8 %shard_map.102 = (bf16[16,1536]{1,0:T(8,128)(2,1)}, bf16[16,1536]{1,0:T(8,128)(2,1)}, bf16[1536,768]{1,0:T(8,128)(2,1)}, bf16[768,1536]{1,0:T(8,128)(2,1)}) custom-call(bf16[16,1536]{1,0:T(8,128)(2,1)} %tok.1, bf16[16,1536]{1,0:T(8,128)(2,1)} %cot.1, bf16[1536,768]{1,0:T(8,128)(2,1)} %up.1, bf16[768,1536]{1,0:T(8,128)(2,1)} %dn.1, s32[6,12]{1,0:T(8,128)} %bitcast.1, ...), custom_call_target="tpu_custom_call" | custom-call | tf_op jit(solution)/shard_map/pallas_call | solution.py:503
  98.5 147.2 %shard_map.103 = (bf16[16,1536]{1,0:T(8,128)(2,1)}, bf16[16,1536]{1,0:T(8,128)(2,1)}, bf16[1536,768]{1,0:T(8,128)(2,1)}, bf16[768,1536]{1,0:T(8,128)(2,1)}) custom-call(bf16[16,1536]{1,0:T(8,128)(2,1)} %get-tuple-element.8.refs_0_, bf16[16,1536]{1,0:T(8,128)(2,1)} %get-tuple-element.9.refs_1_, bf16[1536,768]{1,0:T(8,128)(2,1)} %get-tuple-element.10.refs_2_, ...), custom_call_target="tpu_custom_call" | custom-call | tf_op jit(solution)/shard_map/pallas_call | solution.py:550

commit v3 on v2

--- a/solution.py
+++ b/solution.py
@@ -435,8 +435,6 @@
     ro.pair_wait(0)
     ro.pair_wait(1)
     ro.along_x()
-    ro.relay()
-    ro.near()
 
     gather_wait(3, pg)
     for m in range(2):
@@ -445,16 +443,18 @@
     for e in range(EX):
         sq_a[e : e + 1, :] = jnp.full((1, BLK), norm_up(e) + down_sq[e])
     sq_send(0)
-    ro.along_z()
     ri.pair_wait(0)
     ri.pair_wait(1)
     ri.along_x()
+    ro.relay()
+    ro.near()
     ri.relay()
+    ro.along_z()
+    ri.near()
     sq_sum(0)
     sq_send(1)
+    ri.along_z()
     ro.result(out_o, loc_sem.at[4])
-    ri.near()
-    ri.along_z()
     sq_sum(1)
     scale()
     update_up()
@@ -468,18 +468,26 @@
 
 def settle(*refs):
     sem = refs[-1]
-    copies = []
+    moves = []
     for i in range(4):
-        src, dst = refs[i], refs[4 + i]
+        src, dst, held = refs[i], refs[4 + i], refs[8 + i]
         pieces = 1 if src.shape[0] < 64 else 6
         step = src.shape[0] // pieces
         for p in range(pieces):
-            at = pl.ds(p * step, step)
-            copies.append(pltpu.make_async_copy(src.at[at], dst.at[at], sem.at[len(copies)]))
-    for cp in copies:
-        cp.start()
-    for cp in copies:
-        cp.wait()
+            at, k = pl.ds(p * step, step), len(moves)
+            moves.append(
+                (
+                    pltpu.make_async_copy(src.at[at], held.at[at], sem.at[0, k]),
+                    pltpu.make_async_copy(held.at[at], dst.at[at], sem.at[1, k]),
+                )
+            )
+    for get, _ in moves:
+        get.start()
+    for get, put in moves:
+        get.wait()
+        put.start()
+    for _, put in moves:
+        put.wait()
 
 
 def solution(mesh):
@@ -552,7 +560,7 @@
             out_shape=shapes,
             in_specs=[any_] * 4,
             out_specs=(any_,) * 4,
-            scratch_shapes=[dma((16,))],
+            scratch_shapes=[pltpu.VMEM(t.shape, BF16) for t in shapes] + [dma((2, 16))],
             compiler_params=pltpu.CompilerParams(vmem_limit_bytes=60 * 1024 * 1024),
         )(*made)
 

time: 247 us -> 105 us (0.43)
  the two profiles are of different devices: /device:TPU:1 before, /device:TPU:18 now
where the time goes in v3:
time: 105 us
  Pallas kernels  104 us (99%)
    pallas_call x1, Pallas kernels, local(): pl.pallas_call(functools.partial(kernel, nz, nc), out_shape=shapes, in_sp...  99.6 us
    pallas_call x1, Pallas kernels, local(): pl.pallas_call(settle, out_shape=shapes, in_specs=[any_] * 4, out_specs=(...  4.48 us

profile of v3, /device:TPU:18, one launch (start us, length us, event | category | flops | bytes accessed | tf_op | source)
XLA Modules:
  0.0 104.9 jit_solution(5735617863347519806)
XLA Ops:
  0.6 99.6 %shard_map.102 = (bf16[16,1536]{1,0:T(8,128)(2,1)}, bf16[16,1536]{1,0:T(8,128)(2,1)}, bf16[1536,768]{1,0:T(8,128)(2,1)}, bf16[768,1536]{1,0:T(8,128)(2,1)}) custom-call(bf16[16,1536]{1,0:T(8,128)(2,1)} %tok.1, bf16[16,1536]{1,0:T(8,128)(2,1)} %cot.1, bf16[1536,768]{1,0:T(8,128)(2,1)} %up.1, bf16[768,1536]{1,0:T(8,128)(2,1)} %dn.1, s32[6,12]{1,0:T(8,128)} %bitcast.1, ...), custom_call_target="tpu_custom_call" | custom-call | tf_op jit(solution)/shard_map/pallas_call | solution.py:511
  100.2 4.5 %shard_map.103 = (bf16[16,1536]{1,0:T(8,128)(2,1)}, bf16[16,1536]{1,0:T(8,128)(2,1)}, bf16[1536,768]{1,0:T(8,128)(2,1)}, bf16[768,1536]{1,0:T(8,128)(2,1)}) custom-call(bf16[16,1536]{1,0:T(8,128)(2,1)} %get-tuple-element.8.refs_0_, bf16[16,1536]{1,0:T(8,128)(2,1)} %get-tuple-element.9.refs_1_, bf16[1536,768]{1,0:T(8,128)(2,1)} %get-tuple-element.10.refs_2_, ...), custom_call_target="tpu_custom_call" | custom-call | tf_op jit(solution)/shard_map/pallas_call | solution.py:558

commit v4 on v2

--- a/solution.py
+++ b/solution.py
@@ -30,12 +30,12 @@
 
 def kernel(
     nz, nc,
-    tok, cot, up, dn, upk, dnk, clip,
-    out_o, ing_o, up_o, dn_o,
+    tok, cot, up, dn, upk, dnk,
+    out_o, ing_o, tok_o, cot_o, hid_o, pg_o, mu_o, md_o, sq_o,
     tokp, cotp, upm, dnm, mu, md,
-    send_h, recv_h, hid, pg, dact,
+    send_h, via_x, via_y, from_x, from_y, sum_x, sum_y, hid, pg, dact,
     part, pair, pair_r, row_out, row_in, near_out, near_in, fin, res,
-    sq_a, sq_s, sq_r, psc, csc, uo, do,
+    sq_a, sq_s, sq_r,
     loc_sem, ag_s, ag_r, col_s, col_r, row_s, row_r, sq_ss, sq_rs,
 ):
     tokens = tok.shape[0] * 4 * nz
@@ -58,9 +58,6 @@
 
     def z_at(k):
         return (row_of(x, zmod(z + k), core), c)
-
-    def c_at(k):
-        return (r, lax.rem(c + k, nc))
 
     up_in = pltpu.make_async_copy(up, upm, loc_sem.at[0])
     dn_in = pltpu.make_async_copy(dn, dnm, loc_sem.at[1])
@@ -216,54 +213,137 @@
     per = chunk // blk
     n_chunk = tokens // chunk
 
-    def col_send(a, src, dst, q, k):
-        return send(src, dst, col_s.at[a, k], col_r.at[a, k], (r, q))
-
-    def scatter_chunk(a, m, value):
-        for b in range(per):
-            send_h[a, m * per + b] = value[b * blk : (b + 1) * blk].astype(BF16)
-
-    def scatter_send(a):
-        for k in range(1, nc):
-            q = lax.rem(c + k, nc)
-            col_send(a, send_h.at[a, q], recv_h.at[a, k], q, k)
-
-    def scatter_sum(a):
-        total = send_h[a, c].astype(F32)
-        for k in range(1, nc):
-            arrived(recv_h.at[a, k], col_r.at[a, k], c_at(nc - k))
-            total += recv_h[a, k].astype(F32)
-        return total
-
-    def gather_send(a, panel):
-        for k in range(1, nc):
-            col_send(a, panel.at[c], panel.at[c], lax.rem(c + k, nc), k)
-
-    def gather_wait(a, panel):
-        for k in range(1, nc):
-            q = lax.rem(c + nc - k, nc)
-            arrived(panel.at[q], col_r.at[a, k], (r, q))
+    low, high = pl.ds(0, blk // 2), pl.ds(blk // 2, blk // 2)
+    ny = nc // 2
+    y, xh = lax.div(c, 2), lax.rem(c, 2)
+    ys = range(1, ny)
+
+    def col(j, flip=0):
+        return lax.rem(y + j + ny, ny) * 2 + (1 - xh if flip else xh)
+
+    col_x = (r, col(0, 1))
+
+    def col_y(j):
+        return (r, col(j))
+
+    class Col:
+        def __init__(self, a):
+            self.a, self.keys = a, {}
+
+        def sems(self, key):
+            k = self.keys.setdefault(key, len(self.keys))
+            return col_s.at[self.a, k], col_r.at[self.a, k]
+
+        def put(self, src, dst, key, dev):
+            send(src, dst, *self.sems(key), dev)
+
+        def take(self, dst, key):
+            arrived(dst, self.sems(key)[1], col_x)
+
+    class ColSum(Col):
+        def chunk(self, m, value):
+            for b in range(per):
+                send_h[self.a, m * per + b] = value[b * blk : (b + 1) * blk].astype(BF16)
+
+        def first(self):
+            a = self.a
+            for j in ys:
+                self.put(send_h.at[a, col(j, 1), low], via_y.at[a, j], ("vy", j), col_y(j))
+                self.put(send_h.at[a, col(j, 1), high], via_x.at[a, j], ("vx", j), col_x)
+            for j in ys:
+                self.put(send_h.at[a, col(j), low], from_y.at[a, j, low], ("oy", j), col_y(j))
+            self.put(send_h.at[a, col(0, 1), high], from_x.at[a, high], "ox", col_x)
+
+        def second(self):
+            a = self.a
+            for j in ys:
+                self.take(via_x.at[a, j], ("vx", j))
+                val = send_h[a, col(j), high, :].astype(F32) + via_x[a, j].astype(F32)
+                sum_y[a, j] = val.astype(BF16)
+                self.put(sum_y.at[a, j], from_y.at[a, j, high], ("sy", j), col_y(j))
+            val = send_h[a, col(0, 1), low, :].astype(F32)
+            for j in ys:
+                self.take(via_y.at[a, j], ("vy", j))
+                val += via_y[a, j].astype(F32)
+            sum_x[a] = val.astype(BF16)
+            self.put(sum_x.at[a], from_x.at[a, low], "sx", col_x)
+
+        def total(self):
+            a = self.a
+            self.take(from_x.at[a, high], "ox")
+            self.take(from_x.at[a, low], "sx")
+            val = send_h[a, c].astype(F32) + from_x[a].astype(F32)
+            for j in ys:
+                self.take(from_y.at[a, j, low], ("oy", j))
+                self.take(from_y.at[a, j, high], ("sy", j))
+                val += from_y[a, j].astype(F32)
+            return val
+
+    class ColGather(Col):
+        def __init__(self, a, panel):
+            Col.__init__(self, a)
+            self.panel = panel
+
+        def first(self):
+            own = self.panel.at[c]
+            self.put(own, own, "x", col_x)
+            for j in ys:
+                self.put(own, own, ("y", j), col_y(j))
+
+        def second(self):
+            ref = self.panel.at[col(0, 1)]
+            self.take(ref, "x")
+            ref = self.panel.at[col(0, 1), low]
+            for j in ys:
+                self.put(ref, ref, ("xy", j), col_y(j))
+            for j in ys:
+                self.take(self.panel.at[col(-j)], ("y", j))
+                ref = self.panel.at[col(-j), high]
+                self.put(ref, ref, ("yx", j), col_x)
+
+        def last(self):
+            for j in ys:
+                self.take(self.panel.at[col(-j, 1), low], ("xy", j))
+                self.take(self.panel.at[col(-j, 1), high], ("yx", j))
+
+    s_pre, s_grad = ColSum(0), ColSum(1)
+    g_act, g_pre = ColGather(2, hid), ColGather(3, pg)
+    keeps = []
+
+    def keep(src, dst, k):
+        cp = pltpu.make_async_copy(src, dst, loc_sem.at[8 + k])
+        cp.start()
+        keeps.append(cp)
 
     for m in range(n_chunk):
-        scatter_chunk(0, m, dot(tokp[m * chunk : (m + 1) * chunk], upm[...], 1, 0))
-    scatter_send(0)
+        s_pre.chunk(m, dot(tokp[m * chunk : (m + 1) * chunk], upm[...], 1, 0))
+    s_pre.first()
+    keep(tokp, tok_o, 0)
+    keep(mu, mu_o, 1)
+    keep(md, md_o, 2)
 
     gc.far()
+    s_pre.second()
     gc.finish()
+    keep(cotp, cot_o, 3)
 
     for m in range(n_chunk):
-        scatter_chunk(1, m, dot(cotp[m * chunk : (m + 1) * chunk], dnm[...], 1, 1))
-    scatter_send(1)
-
-    v = scatter_sum(0)
+        s_grad.chunk(m, dot(cotp[m * chunk : (m + 1) * chunk], dnm[...], 1, 1))
+    s_grad.first()
+
+    v = s_pre.total()
     t = jnp.tanh(ROOT * (v + 0.044715 * (v * v * v)))
     hid[c] = (0.5 * v * (1.0 + t)).astype(BF16)
-    gather_send(2, hid)
+    g_act.first()
     dact[...] = 0.5 * (1.0 + t) + (0.5 * ROOT) * v * (1.0 - t * t) * (1.0 + 0.134145 * (v * v))
 
-    g = scatter_sum(1)
+    s_grad.second()
+    g_act.second()
+    g = s_grad.total()
     pg[c] = (g * dact[...]).astype(BF16)
-    gather_send(3, pg)
+    g_pre.first()
+    g_act.last()
+    keep(hid, hid_o, 4)
 
     outs = []
 
@@ -391,94 +471,105 @@
             total += sq_r[g, k]
         sq_a[...] = total
 
-    tile = 256
-
-    def scale():
-        for e in range(EX):
-            total = sq_a[e : e + 1, :]
-            bound = clip[e].astype(F32) * BOUND
-            f = jnp.minimum(1.0, bound / jnp.sqrt(total + 1e-6))[:, 0:1]
-            psc[e * SEQ : (e + 1) * SEQ] = (example(pg, e).astype(F32) * f).astype(BF16)
-            at = slice(e * SEQ, (e + 1) * SEQ)
-            csc[at] = (cotp[at].astype(F32) * f).astype(BF16)
-
-    def update_up():
-        for i in range(width // tile):
-            at = slice(i * tile, (i + 1) * tile)
-            g2 = dot(tokp[:, at], psc[...], 0, 0)
-            for h in range(tile // BLK):
-                lo = i * tile + h * BLK
-                row = mu[lo // BLK : lo // BLK + 1, :] * UNIT
-                uo[lo : lo + BLK, :] = (g2[h * BLK : (h + 1) * BLK] * row).astype(BF16)
-            cp = pltpu.make_async_copy(uo.at[at], up_o.at[at], loc_sem.at[6 + i])
-            cp.start()
-            outs.append(cp)
-
-    def update_down():
-        hf = hid[...].reshape(tokens, hidden)
-        for i in range(hidden // tile):
-            at = slice(i * tile, (i + 1) * tile)
-            g2 = dot(hf[:, at], csc[...], 0, 0)
-            for h in range(tile // BLK):
-                lo = i * tile + h * BLK
-                row = md[lo // BLK : lo // BLK + 1, :] * UNIT
-                do[lo : lo + BLK, :] = (g2[h * BLK : (h + 1) * BLK] * row).astype(BF16)
-            cp = pltpu.make_async_copy(do.at[at], dn_o.at[at], loc_sem.at[6 + width // tile + i])
-            cp.start()
-            outs.append(cp)
-
     ro, ri = RowSum(0), RowSum(1)
-    gather_wait(2, hid)
-    for m in range(2):
-        ro.rows_of(m, dot(flat(hid, m), dnm[...], 1, 0))
+    ro.rows_of(0, dot(flat(hid, 0), dnm[...], 1, 0))
+    g_pre.second()
+    ro.rows_of(1, dot(flat(hid, 1), dnm[...], 1, 0))
     down_sq = [norm_down(e) for e in range(EX)]
     ro.pair_wait(0)
     ro.pair_wait(1)
     ro.along_x()
-    ro.relay()
-    ro.near()
-
-    gather_wait(3, pg)
+
+    g_pre.last()
+    keep(pg, pg_o, 5)
     for m in range(2):
         ri.rows_of(m, dot(flat(pg, m), upm[...], 1, 1))
     sq_a[...] = jnp.zeros_like(sq_a)
     for e in range(EX):
         sq_a[e : e + 1, :] = jnp.full((1, BLK), norm_up(e) + down_sq[e])
     sq_send(0)
-    ro.along_z()
     ri.pair_wait(0)
     ri.pair_wait(1)
     ri.along_x()
-    ri.relay()
+    ro.relay()
+    ro.near()
     sq_sum(0)
     sq_send(1)
-    ro.result(out_o, loc_sem.at[4])
+    ri.relay()
+    ro.along_z()
     ri.near()
     ri.along_z()
+    ro.result(out_o, loc_sem.at[4])
     sq_sum(1)
-    scale()
-    update_up()
-    update_down()
+    keep(sq_a, sq_o, 6)
     ri.result(ing_o, loc_sem.at[5])
-    for cp in outs:
+    for cp in outs + keeps:
         cp.wait()
     for copy in pending:
         copy.wait_send()
 
 
-def settle(*refs):
-    sem = refs[-1]
-    copies = []
-    for i in range(4):
-        src, dst = refs[i], refs[4 + i]
-        pieces = 1 if src.shape[0] < 64 else 6
-        step = src.shape[0] // pieces
-        for p in range(pieces):
-            at = pl.ds(p * step, step)
-            copies.append(pltpu.make_async_copy(src.at[at], dst.at[at], sem.at[len(copies)]))
-    for cp in copies:
+def update(
+    out_t, ing_t, tok_t, cot_t, hid_t, pg_t, mu_t, md_t, sq_t, clip,
+    out_o, ing_o, up_o, dn_o,
+    out_v, ing_v, tokp, cotp, hid, pg, mu, md, sq, psc, csc, uo, do, sem, put_sem,
+):
+    def get(src, dst, k):
+        cp = pltpu.make_async_copy(src, dst, sem.at[k])
         cp.start()
-    for cp in copies:
+        return cp
+
+    blk = hid_t.shape[1]
+    tokens, width = tok_t.shape
+    hidden = hid_t.shape[2]
+    n = SEQ // blk
+    got = [
+        get(sq_t, sq, 0), get(pg_t, pg, 1), get(mu_t, mu, 2), get(md_t, md, 3),
+        get(tok_t, tokp, 4), get(cot_t, cotp, 5), get(hid_t, hid, 6), get(out_t, out_v, 7), get(ing_t, ing_v, 8),
+    ]
+    puts = []
+
+    def put(src, dst):
+        cp = pltpu.make_async_copy(src, dst, put_sem.at[len(puts)])
+        cp.start()
+        puts.append(cp)
+
+    got[0].wait()
+    got[1].wait()
+    scale = []
+    for e in range(EX):
+        bound = clip[e].astype(F32) * BOUND
+        scale.append(jnp.minimum(1.0, bound / jnp.sqrt(sq[e : e + 1, :] + 1e-6))[:, 0:1])
+        part = pg[e * n : (e + 1) * n].reshape(SEQ, hidden)
+        psc[e * SEQ : (e + 1) * SEQ] = (part.astype(F32) * scale[e]).astype(BF16)
+    for cp in got[2:5]:
+        cp.wait()
+    tile = 256
+    for i in range(width // tile):
+        at = slice(i * tile, (i + 1) * tile)
+        g2 = dot(tokp[:, at], psc[...], 0, 0)
+        for h in range(tile // BLK):
+            lo = i * tile + h * BLK
+            row = mu[lo // BLK : lo // BLK + 1, :] * UNIT
+            uo[lo : lo + BLK, :] = (g2[h * BLK : (h + 1) * BLK] * row).astype(BF16)
+        put(uo.at[at], up_o.at[at])
+    for cp in got[5:]:
+        cp.wait()
+    put(out_v, out_o)
+    put(ing_v, ing_o)
+    for e in range(EX):
+        at = slice(e * SEQ, (e + 1) * SEQ)
+        csc[at] = (cotp[at].astype(F32) * scale[e]).astype(BF16)
+    hf = hid[...].reshape(tokens, hidden)
+    for i in range(hidden // tile):
+        at = slice(i * tile, (i + 1) * tile)
+        g2 = dot(hf[:, at], csc[...], 0, 0)
+        for h in range(tile // BLK):
+            lo = i * tile + h * BLK
+            row = md[lo // BLK : lo // BLK + 1, :] * UNIT
+            do[lo : lo + BLK, :] = (g2[h * BLK : (h + 1) * BLK] * row).astype(BF16)
+        put(do.at[at], dn_o.at[at])
+    for cp in puts:
         cp.wait()
 
 
@@ -494,17 +585,17 @@
         dma = pltpu.SemaphoreType.DMA
         n_ag = 32
         n_row = 2 + len(ROW_KEYS)
-        shapes = (
-            jax.ShapeDtypeStruct(tok.shape, BF16),
-            jax.ShapeDtypeStruct(tok.shape, BF16),
-            jax.ShapeDtypeStruct(up.shape, BF16),
-            jax.ShapeDtypeStruct(dn.shape, BF16),
-        )
+        panel = jax.ShapeDtypeStruct((tokens, width), BF16)
+        rowed = jax.ShapeDtypeStruct((nc, blk, hidden), BF16)
+        shard = jax.ShapeDtypeStruct(tok.shape, BF16)
+        up_mask = jax.ShapeDtypeStruct((16, hidden), F32)
+        down_mask = jax.ShapeDtypeStruct((8, width), F32)
+        squares = jax.ShapeDtypeStruct((8, BLK), F32)
         made = pl.pallas_call(
             functools.partial(kernel, nz, nc),
-            out_shape=shapes,
-            in_specs=[any_] * 4 + [sm] * 3,
-            out_specs=(any_,) * 4,
+            out_shape=(shard, shard, panel, panel, rowed, rowed, up_mask, down_mask, squares),
+            in_specs=[any_] * 4 + [sm] * 2,
+            out_specs=(any_,) * 9,
             scratch_shapes=[
                 pltpu.VMEM((tokens, width), BF16),
                 pltpu.VMEM((tokens, width), BF16),
@@ -513,7 +604,12 @@
                 pltpu.VMEM((16, hidden), F32),
                 pltpu.VMEM((8, width), F32),
                 pltpu.VMEM((2, nc, blk, hidden), BF16),
-                pltpu.VMEM((2, nc, blk, hidden), BF16),
+                pltpu.VMEM((2, nc // 2, blk // 2, hidden), BF16),
+                pltpu.VMEM((2, nc // 2, blk // 2, hidden), BF16),
+                pltpu.VMEM((2, blk, hidden), BF16),
+                pltpu.VMEM((2, nc // 2, blk, hidden), BF16),
+                pltpu.VMEM((2, blk // 2, hidden), BF16),
+                pltpu.VMEM((2, nc // 2, blk // 2, hidden), BF16),
                 pltpu.VMEM((nc, blk, hidden), BF16),
                 pltpu.VMEM((nc, blk, hidden), BF16),
                 pltpu.VMEM((blk, hidden), F32),
@@ -529,15 +625,11 @@
                 pltpu.VMEM((8, BLK), F32),
                 pltpu.VMEM((2, 8, BLK), F32),
                 pltpu.VMEM((2, 16, 8, BLK), F32),
-                pltpu.VMEM((tokens, hidden), BF16),
-                pltpu.VMEM((tokens, width), BF16),
-                pltpu.VMEM((width, hidden), BF16),
-                pltpu.VMEM((hidden, width), BF16),
-                dma((24,)),
+                dma((16,)),
                 dma((2, n_ag)),
                 dma((2, n_ag)),
-                dma((4, nc)),
-                dma((4, nc)),
+                dma((4, 16)),
+                dma((4, 16)),
                 dma((2, n_row)),
                 dma((2, n_row)),
                 dma((2, 16)),
@@ -546,15 +638,19 @@
             compiler_params=pltpu.CompilerParams(
                 collective_id=0, has_side_effects=True, vmem_limit_bytes=56 * 1024 * 1024
             ),
-        )(tok, cot, up, dn, upk.T, dnk, clip)
+        )(tok, cot, up, dn, upk.T, dnk)
+        grad_up = jax.ShapeDtypeStruct(up.shape, BF16)
+        grad_dn = jax.ShapeDtypeStruct(dn.shape, BF16)
+        held = (shard, shard, panel, panel, rowed, rowed, up_mask, down_mask, squares)
+        held += (jax.ShapeDtypeStruct((tokens, hidden), BF16), panel, grad_up, grad_dn)
         return pl.pallas_call(
-            settle,
-            out_shape=shapes,
-            in_specs=[any_] * 4,
+            update,
+            out_shape=(shard, shard, grad_up, grad_dn),
+            in_specs=[any_] * 9 + [sm],
             out_specs=(any_,) * 4,
-            scratch_shapes=[dma((16,))],
+            scratch_shapes=[pltpu.VMEM(t.shape, t.dtype) for t in held] + [dma((16,)), dma((16,))],
             compiler_params=pltpu.CompilerParams(vmem_limit_bytes=60 * 1024 * 1024),
-        )(*made)
+        )(*made, clip)
 
     placed = (
         P("row", "col"),

time: 247 us -> 98 us (0.40)
  Pallas kernels: 245 us -> 97 us
    pallas_call x2, Pallas kernels: 245 us -> 97 us  [the longest x1 90.6 us: local(): pl.pallas_call(functools.partial(kernel, nz, nc), out_shape=(shard, shard...]
where the time goes in v4:
time: 98 us; the launch traced here: 97.8 us
  Pallas kernels  97 us (99%)
    pallas_call x1, Pallas kernels, local(): pl.pallas_call(functools.partial(kernel, nz, nc), out_shape=(shard, shard...  90.6 us
    pallas_call x1, Pallas kernels, local(): pl.pallas_call(update, out_shape=(shard, shard, grad_up, grad_dn), in_spe...  6.38 us

profile of v4, /device:TPU:1, one launch (start us, length us, event | category | flops | bytes accessed | tf_op | source)
XLA Modules:
  0.0 97.8 jit_solution(9061309340865417728)
XLA Ops:
  0.6 90.6 %shard_map.102 = (bf16[16,1536]{1,0:T(8,128)(2,1)}, bf16[16,1536]{1,0:T(8,128)(2,1)}, bf16[512,1536]{1,0:T(8,128)(2,1)}, bf16[512,1536]{1,0:T(8,128)(2,1)}, bf16...) custom-call(bf16[16,1536]{1,0:T(8,128)(2,1)} %tok.1, ...), custom_call_target="tpu_custom_call" | custom-call | tf_op jit(solution)/shard_map/pallas_call | solution.py:594
  91.3 6.4 %shard_map.103 = (bf16[16,1536]{1,0:T(8,128)(2,1)}, bf16[16,1536]{1,0:T(8,128)(2,1)}, bf16[1536,768]{1,0:T(8,128)(2,1)}, bf16[768,1536]{1,0:T(8,128)(2,1)}) custom-call(bf16[16,1536]{1,0:T(8,128)(2,1)} %get-tuple-element.13.out_t, bf16[16,1536]{1,0:T(8,128)(2,1)} %get-tuple-element.14.ing_t, bf16[512,1536]{1,0:T(8,128)(2,1)} %get-tuple-element.15.tok_t, ...), custom_call_target="tpu_custom_call" | custom-call | tf_op jit(solution)/shard_map/pallas_call | solution.py:646

commit v5 on v4

v5 whole, which is shorter than its diff:
```python
import functools
import math

import jax
import jax.numpy as jnp
from jax import lax
from jax.experimental import pallas as pl
from jax.experimental.pallas import tpu as pltpu
from jax.sharding import PartitionSpec as P

MESH = pl.DeviceIdType.MESH
D = 12288
FF = 24576
SEQ = 128
BLK = 128
EX = 4
SUB = 16
F32 = jnp.float32
BF16 = jnp.bfloat16
ROOT = math.sqrt(2.0 / math.pi)
ROW_KEYS = [("x", 4), ("x", 3), ("x", -3), ("x", 2), ("x", -2), ("x", 0), ("n", 1), ("n", -1)]
ROW_KEYS += [("r", 4), ("r", 3), ("r", -3), ("z", 2), ("z", -2)]
UNIT = 7.0 / (EX * math.sqrt(SEQ))
BOUND = math.sqrt(D * FF * SEQ) / 1000.0


def dot(a, b, ca, cb):
    return lax.dot_general(a, b, (((ca,), (cb,)), ((), ())), preferred_element_type=F32)


def kernel(
    nz, nc,
    tok, cot, up, dn, upk, dnk, clip,
    out_o, ing_o, tok_o, cot_o, hid_o, pg_o, mu_o, md_o, fac_o,
    tokp, cotp, upm, dnm, mu, md,
    send_h, via_x, via_y, from_x, from_y, sum_x, sum_y, hid, pg, dact,
    part, pair, pair_r, row_out, row_in, near_out, near_in, fin, res,
    sq_a, sq_s, sq_r, fac,
    loc_sem, ag_s, ag_r, col_s, col_r, row_s, row_r, sq_ss, sq_rs,
):
    tokens = tok.shape[0] * 4 * nz
    width = tok.shape[1]
    hidden = up.shape[1]
    r = lax.axis_index("row")
    c = lax.axis_index("col")
    core = lax.rem(r, 2)
    z = lax.rem(lax.div(r, 2), nz)
    x = lax.div(r, 2 * nz)

    def row_of(xx, zz, kk):
        return (xx * nz + zz) * 2 + kk

    def zmod(v):
        return lax.rem(v + 2 * nz, nz)

    core_dev = (row_of(x, z, 1 - core), c)
    x_dev = (row_of(1 - x, z, core), c)

    def z_at(k):
        return (row_of(x, zmod(z + k), core), c)

    up_in = pltpu.make_async_copy(up, upm, loc_sem.at[0])
    dn_in = pltpu.make_async_copy(dn, dnm, loc_sem.at[1])
    up_in.start()
    dn_in.start()

    def place(off):
        return (off + 1) % nz

    own = [
        pltpu.make_async_copy(tok, tokp.at[place(0), 0, 0], loc_sem.at[2]),
        pltpu.make_async_copy(cot, cotp.at[place(0), 0, 0], loc_sem.at[3]),
    ]
    own[0].start()
    own[1].start()

    barrier = pltpu.get_barrier_semaphore()
    near_c = [(0, 1)] + [(k, kk) for k in range(1, nc) for kk in (0, 1)]
    near_z = [(0, 1)] + [(k, m) for k in range(1, nz) for m in (0, 1)]

    def cc_at(k, kk):
        return (row_of(x, z, core if kk == 0 else 1 - core), lax.rem(c + k, nc))

    def xz_at(k, m):
        return (row_of(x if m == 0 else 1 - x, zmod(z + k), core), c)

    peers = [cc_at(*p) for p in near_c] + [xz_at(*p) for p in near_z]
    for dev in peers:
        pl.semaphore_signal(barrier, inc=1, device_id=dev, device_id_type=MESH)
    pl.semaphore_wait(barrier, len(peers))
    own[0].wait()
    own[1].wait()

    pending = []

    def send(src, dst, ssem, rsem, dev):
        copy = pltpu.make_async_remote_copy(
            src_ref=src, dst_ref=dst, send_sem=ssem, recv_sem=rsem, device_id=dev, device_id_type=MESH
        )
        copy.start()
        pending.append(copy)
        return copy

    def arrived(dst, rsem, dev):
        pltpu.make_async_remote_copy(
            src_ref=dst, dst_ref=dst, send_sem=rsem, recv_sem=rsem, device_id=dev, device_id_type=MESH
        ).wait_recv()

    class Gather:
        def __init__(self, a, shard, panel):
            self.a, self.shard, self.panel, self.keys = a, shard, panel, {}

        def sems(self, key):
            k = self.keys.setdefault(key, len(self.keys))
            return ag_s.at[self.a, k], ag_r.at[self.a, k]

        def slot(self, stream, off, other=0):
            return self.panel.at[place(off), stream, other]

        def z_put(self, stream, off, hop, key):
            src, dst = self.slot(stream, off), self.slot(stream, off - hop)
            send(src, dst, *self.sems(key), z_at(hop))

        def take(self, stream, off, key):
            arrived(self.slot(stream, off), self.sems(key)[1], x_dev)

        def core_put(self, stream, off):
            src, dst = self.slot(stream, off), self.slot(stream, off, 1)
            send(src, dst, *self.sems(("core", stream, off % nz)), core_dev)

        def x_put(self, off):
            send(self.slot(0, off), self.slot(1, off), *self.sems(("x", off % nz)), x_dev)

        def start(self):
            for sign in (1, -1):
                self.z_put(0, 0, sign, ("z", 0, sign))
                self.z_put(0, 0, 2 * sign, ("z", 0, 2 * sign))
            self.x_put(0)
            self.core_put(0, 0)

        def partner(self):
            self.take(1, 0, ("x", 0))
            for sign in (1, -1):
                self.z_put(1, 0, sign, ("z", 1, sign))
            self.core_put(1, 0)

        def near(self):
            for sign in (-1, 1):
                self.take(0, -2 * sign, ("z", 0, 2 * sign))
                self.x_put(-2 * sign)
                self.z_put(0, -2 * sign, sign, ("z", 0, 3 * sign))
                if sign == (1, -1)[self.a]:
                    self.z_put(0, -2 * sign, 2 * sign, ("z", 0, 4))
                self.core_put(0, -2 * sign)
            for sign in (1, -1):
                self.take(0, -sign, ("z", 0, sign))
                self.core_put(0, -sign)

        def near_done(self):
            for sign in (1, -1):
                self.take(1, -sign, ("z", 1, sign))
                self.core_put(1, -sign)
            self.take(1, 2, ("x", 2))
            self.core_put(1, 2)
            self.core_wait((-1, 0, 1, 2))

        def far(self):
            for sign in (1, -1):
                self.take(0, -3 * sign, ("z", 0, 3 * sign))
                self.x_put(-3 * sign)
                self.core_put(0, -3 * sign)
            self.take(0, 4, ("z", 0, 4))
            self.x_put(4)
            self.core_put(0, 4)

        def far_done(self):
            for off in (-2, 3, -3, 4):
                self.take(1, off, ("x", off % nz))
                self.core_put(1, off)
            self.core_wait((-2, 3, -3, 4))

        def core_wait(self, offs):
            for stream in (0, 1):
                for off in offs:
                    key = ("core", stream, off % nz)
                    arrived(self.slot(stream, off, 1), self.sems(key)[1], core_dev)

    gt = Gather(0, tok, tokp)
    gc = Gather(1, cot, cotp)
    gt.start()
    gt.partner()
    gt.near()
    gc.start()

    nbu, nbh = width // BLK, hidden // BLK
    for i in range(nbu):
        for j in range(nbh):
            mu[i : i + 1, j * BLK : (j + 1) * BLK] = jnp.full((1, BLK), upk[j, i].astype(F32))
            md[j : j + 1, i * BLK : (i + 1) * BLK] = jnp.full((1, BLK), dnk[j, i].astype(F32))
    up_in.wait()

    @pl.loop(0, nbu)
    def _(i):
        at = pl.ds(pl.multiple_of(i * BLK, BLK), BLK)
        upm[at, :] = upm[at, :] * mu[pl.ds(i, 1), :].astype(BF16)

    dn_in.wait()

    @pl.loop(0, nbh)
    def _(j):
        at = pl.ds(pl.multiple_of(j * BLK, BLK), BLK)
        dnm[at, :] = dnm[at, :] * md[pl.ds(j, 1), :].astype(BF16)

    chunk = tokens // 2
    blk = chunk // nc
    low, high = pl.ds(0, blk // 2), pl.ds(blk // 2, blk // 2)
    ny = nc // 2
    y, xh = lax.div(c, 2), lax.rem(c, 2)
    ys = range(1, ny)
    NEAR, FAR = 0, 1

    def half(ref, ch):
        n = nz // 2
        return ref[ch * n : (ch + 1) * n].reshape(chunk, ref.shape[-1])

    def col(j, flip=0):
        return lax.rem(y + j + ny, ny) * 2 + (1 - xh if flip else xh)

    col_x = (r, col(0, 1))

    def col_y(j):
        return (r, col(j))

    class Col:
        def __init__(self, a):
            self.a, self.keys = a, {}

        def sems(self, key):
            k = self.keys.setdefault(key, len(self.keys))
            return col_s.at[self.a, k], col_r.at[self.a, k]

        def put(self, src, dst, key, dev):
            send(src, dst, *self.sems(key), dev)

        def take(self, dst, key):
            arrived(dst, self.sems(key)[1], col_x)

    class ColSum(Col):
        def first(self, value):
            a = self.a
            for b in range(nc):
                send_h[a, b] = value[b * blk : (b + 1) * blk].astype(BF16)
            for j in ys:
                self.put(send_h.at[a, col(j, 1), low], via_y.at[a, j], ("vy", j), col_y(j))
                self.put(send_h.at[a, col(j, 1), high], via_x.at[a, j], ("vx", j), col_x)
            for j in ys:
                self.put(send_h.at[a, col(j), low], from_y.at[a, j, low], ("oy", j), col_y(j))
            self.put(send_h.at[a, col(0, 1), high], from_x.at[a, high], "ox", col_x)

        def second(self):
            a = self.a
            for j in ys:
                self.take(via_x.at[a, j], ("vx", j))
                val = send_h[a, col(j), high, :].astype(F32) + via_x[a, j].astype(F32)
                sum_y[a, j] = val.astype(BF16)
                self.put(sum_y.at[a, j], from_y.at[a, j, high], ("sy", j), col_y(j))
            val = send_h[a, col(0, 1), low, :].astype(F32)
            for j in ys:
                self.take(via_y.at[a, j], ("vy", j))
                val += via_y[a, j].astype(F32)
            sum_x[a] = val.astype(BF16)
            self.put(sum_x.at[a], from_x.at[a, low], "sx", col_x)

        def total(self):
            a = self.a
            self.take(from_x.at[a, high], "ox")
            self.take(from_x.at[a, low], "sx")
            val = send_h[a, c].astype(F32) + from_x[a].astype(F32)
            for j in ys:
                self.take(from_y.at[a, j, low], ("oy", j))
                self.take(from_y.at[a, j, high], ("sy", j))
                val += from_y[a, j].astype(F32)
            return val

    class ColGather(Col):
        def __init__(self, a, panel, ch):
            Col.__init__(self, a)
            self.panel, self.ch = panel, ch

        def block(self, q, part=None):
            at = (self.ch * (nz // 2) + lax.div(q, 2), lax.rem(q, 2))
            return self.panel.at[at] if part is None else self.panel.at[at + (part,)]

        def first(self, value):
            self.panel[self.ch * (nz // 2) + lax.div(c, 2), lax.rem(c, 2)] = value.astype(BF16)
            own = self.block(c)
            self.put(own, own, "x", col_x)
            for j in ys:
                self.put(own, own, ("y", j), col_y(j))

        def second(self):
            self.take(self.block(col(0, 1)), "x")
            ref = self.block(col(0, 1), low)
            for j in ys:
                self.put(ref, ref, ("xy", j), col_y(j))
            for j in ys:
                self.take(self.block(col(-j)), ("y", j))
                ref = self.block(col(-j), high)
                self.put(ref, ref, ("yx", j), col_x)

        def last(self):
            for j in ys:
                self.take(self.block(col(-j, 1), low), ("xy", j))
                self.take(self.block(col(-j, 1), high), ("yx", j))

    s_pre, s_grad = [ColSum(0), ColSum(1)], [ColSum(2), ColSum(3)]
    g_act = [ColGather(4, hid, NEAR), ColGather(5, hid, FAR)]
    g_pre = [ColGather(6, pg, NEAR), ColGather(7, pg, FAR)]
    keeps = []

    def keep(src, dst, k):
        cp = pltpu.make_async_copy(src, dst, loc_sem.at[8 + k])
        cp.start()
        keeps.append(cp)

    def activate(ch):
        v = s_pre[ch].total()
        t = jnp.tanh(ROOT * (v + 0.044715 * (v * v * v)))
        g_act[ch].first(0.5 * v * (1.0 + t))
        dact[ch] = 0.5 * (1.0 + t) + (0.5 * ROOT) * v * (1.0 - t * t) * (1.0 + 0.134145 * (v * v))

    gt.near_done()
    s_pre[NEAR].first(dot(half(tokp, NEAR), upm[...], 1, 0))
    gt.far()
    gc.partner()
    s_pre[NEAR].second()
    gt.far_done()
    s_pre[FAR].first(dot(half(tokp, FAR), upm[...], 1, 0))
    gc.near()
    keep(tokp, tok_o, 0)
    keep(mu, mu_o, 1)
    keep(md, md_o, 2)
    activate(NEAR)
    s_pre[FAR].second()
    gc.near_done()
    gc.far()
    gc.far_done()
    keep(cotp, cot_o, 3)
    s_grad[FAR].first(dot(half(cotp, FAR), dnm[...], 1, 1))
    s_grad[NEAR].first(dot(half(cotp, NEAR), dnm[...], 1, 1))
    g_act[NEAR].second()
    activate(FAR)
    s_grad[FAR].second()
    s_grad[NEAR].second()
    g_act[FAR].second()
    g_pre[FAR].first(s_grad[FAR].total() * dact[FAR])
    g_pre[NEAR].first(s_grad[NEAR].total() * dact[NEAR])

    outs = []

    class RowSum:
        def __init__(self, a):
            self.a = a

        def sems(self, k):
            return row_s.at[self.a, k], row_r.at[self.a, k]

        def emit(self, ch, value):
            n = nz // 2
            v5 = value.reshape(n, 2, 2, SUB, width)
            part[self.a, ch * n : (ch + 1) * n] = v5[:, :, 0]
            pair[self.a, ch * n : (ch + 1) * n] = v5[:, :, 1]
            at = pl.ds(ch * n, n)
            send(pair.at[self.a, at], pair_r.at[self.a, at], *self.sems(ch), core_dev)

        def pair_wait(self, ch):
            at = pl.ds(ch * (nz // 2), nz // 2)
            arrived(pair_r.at[self.a, at], self.sems(ch)[1], core_dev)

        def q(self, stream, off):
            return part[self.a, place(off), stream] + pair_r[self.a, place(off), stream]

        def key(self, name):
            return self.sems(2 + ROW_KEYS.index(name))

        def out(self, slot, name, dev):
            send(row_out.at[self.a, slot], row_in.at[self.a, slot], *self.key(name), dev)

        def get(self, slot, name):
            arrived(row_in.at[self.a, slot], self.key(name)[1], x_dev)

        def along_x(self, slots):
            for slot in slots:
                off = (4, 3, -3, 2, -2)[slot]
                row_out[self.a, slot] = self.q(1, off).astype(BF16)
                self.out(slot, ("x", off), x_dev)

        def next_door(self):
            for way, sign in ((0, 1), (1, -1)):
                for m in (0, 1):
                    near_out[self.a, way, m] = self.q(m, sign).astype(BF16)
                send(near_out.at[self.a, way], near_in.at[self.a, way], *self.key(("n", sign)), z_at(sign))

        def relay(self):
            sign = (1, -1)[self.a]
            for slot, off, hop in ((0, 4, 2 * sign), (1, 3, 1), (2, -3, -1)):
                self.get(slot, ("x", off))
                val = self.q(0, off) + row_in[self.a, slot].astype(F32)
                row_out[self.a, 5 + slot] = val.astype(BF16)
                self.out(5 + slot, ("r", off), z_at(hop))

        def near(self):
            for way, sign in ((0, 1), (1, -1)):
                arrived(near_in.at[self.a, way], self.key(("n", sign))[1], x_dev)
            for m in (0, 1):
                val = self.q(m, 0)
                for way in (0, 1):
                    val += near_in[self.a, way, m].astype(F32)
                fin[self.a, m] = val
            row_out[self.a, 10] = fin[self.a, 1].astype(BF16)
            self.out(10, ("x", 0), x_dev)

        def along_z(self):
            for way, sign in ((0, 1), (1, -1)):
                self.get(3 + way, ("x", 2 * sign))
                self.get(6 + way, ("r", 3 * sign))
                val = self.q(0, 2 * sign) + row_in[self.a, 3 + way].astype(F32)
                val += row_in[self.a, 6 + way].astype(F32)
                if way == self.a:
                    self.get(5, ("r", 4))
                    val += row_in[self.a, 5].astype(F32)
                row_out[self.a, 8 + way] = val.astype(BF16)
                self.out(8 + way, ("z", 2 * sign), z_at(2 * sign))

        def result(self, o, sem):
            self.get(10, ("x", 0))
            val = fin[self.a, 0] + row_in[self.a, 10].astype(F32)
            for way, sign in ((0, 1), (1, -1)):
                self.get(8 + way, ("z", 2 * sign))
                val += row_in[self.a, 8 + way].astype(F32)
            res[self.a] = val.astype(BF16)
            cp = pltpu.make_async_copy(res.at[self.a], o, sem)
            cp.start()
            outs.append(cp)

    def number(s, h):
        return lax.rem(x + s, 2) * 2 + h

    def example(ref, s, h):
        n = nz // 2
        parts = [ref[zmod(h * n + i - z + 1), s].reshape(SEQ // n, ref.shape[-1]) for i in range(n)]
        return jnp.concatenate(parts, axis=0)

    def norm_down(s, h):
        cote, he = example(cotp, s, h), example(hid, s, h)
        acc = jnp.zeros((1, width), F32)
        for j in range(nbh):
            gg = dot(he[:, j * BLK : (j + 1) * BLK], cote, 0, 0)
            acc += jnp.sum(gg * gg, axis=0, keepdims=True) * md[j : j + 1, :]
        return jnp.sum(acc)

    def norm_up(s, h):
        toke, pge = example(tokp, s, h), example(pg, s, h)
        acc = jnp.zeros((1, hidden), F32)
        for i in range(nbu):
            gg = dot(toke[:, i * BLK : (i + 1) * BLK], pge, 0, 0)
            acc += jnp.sum(gg * gg, axis=0, keepdims=True) * mu[i : i + 1, :]
        return jnp.sum(acc)

    groups = [
        [(cc_at(k, kk), cc_at(nc - k, kk)) for k, kk in near_c],
        [(xz_at(k, m), xz_at(nz - k, m)) for k, m in near_z],
    ]

    def sq_send(g):
        sq_s[g] = sq_a[...]
        for k, (dev, _) in enumerate(groups[g]):
            send(sq_s.at[g], sq_r.at[g, k], sq_ss.at[g, k], sq_rs.at[g, k], dev)

    def sq_sum(g):
        total = sq_a[...]
        for k, (_, dev) in enumerate(groups[g]):
            arrived(sq_r.at[g, k], sq_rs.at[g, k], dev)
            total += sq_r[g, k]
        sq_a[...] = total

    ro, ri = RowSum(0), RowSum(1)
    g_act[NEAR].last()
    g_act[FAR].last()
    keep(hid, hid_o, 4)
    g_pre[FAR].second()
    ro.emit(FAR, dot(half(hid, FAR), dnm[...], 1, 0))
    g_pre[NEAR].second()
    ro.emit(NEAR, dot(half(hid, NEAR), dnm[...], 1, 0))
    g_pre[FAR].last()
    ri.emit(FAR, dot(half(pg, FAR), upm[...], 1, 1))
    ro.pair_wait(FAR)
    ro.along_x((0, 1, 2, 4))
    ri.pair_wait(FAR)
    ri.along_x((0, 1, 2, 4))
    ro.pair_wait(NEAR)
    ro.along_x((3,))
    ro.next_door()
    examples = [(s, h) for s in (0, 1) for h in (0, 1)]
    down_sq = [norm_down(*e) for e in examples]
    ro.relay()

    g_pre[NEAR].last()
    keep(pg, pg_o, 5)
    ri.emit(NEAR, dot(half(pg, NEAR), upm[...], 1, 1))
    sq_a[...] = jnp.zeros_like(sq_a)
    for e, down in zip(examples, down_sq):
        sq_a[pl.ds(number(*e), 1), :] = jnp.full((1, BLK), norm_up(*e) + down)
    sq_send(0)
    ri.pair_wait(NEAR)
    ri.along_x((3,))
    ri.next_door()
    ri.relay()
    ro.near()
    ro.along_z()
    sq_sum(0)
    sq_send(1)
    ri.near()
    ri.along_z()
    ro.result(out_o, loc_sem.at[4])
    sq_sum(1)
    for p in range(nz):
        for s in (0, 1):
            e = lax.rem(x + s, 2) * 2 + lax.div(zmod(z + p - 1), nz // 2)
            bound = clip[e].astype(F32) * BOUND
            f = jnp.minimum(1.0, bound / jnp.sqrt(sq_a[pl.ds(e, 1), :] + 1e-6))
            fac[2 * p + s : 2 * p + s + 1, :] = f
    keep(fac, fac_o, 6)
    ri.result(ing_o, loc_sem.at[5])
    for cp in outs + keeps:
        cp.wait()
    for copy in pending:
        copy.wait_send()


def update(
    out_t, ing_t, tok_t, cot_t, hid_t, pg_t, mu_t, md_t, fac_t,
    out_o, ing_o, up_o, dn_o,
    out_v, ing_v, tokp, cotp, hid, pg, mu, md, fac, psc, csc, uo, do, sem, put_sem,
):
    def get(src, dst, k):
        cp = pltpu.make_async_copy(src, dst, sem.at[k])
        cp.start()
        return cp

    width, hidden = tok_t.shape[-1], hid_t.shape[-1]
    tokens = psc.shape[0]
    n = tok_t.shape[0] * tok_t.shape[1]
    run = tokens // n
    got = [
        get(fac_t, fac, 0), get(pg_t, pg, 1), get(mu_t, mu, 2), get(md_t, md, 3),
        get(tok_t, tokp, 4), get(cot_t, cotp, 5), get(hid_t, hid, 6), get(out_t, out_v, 7), get(ing_t, ing_v, 8),
    ]
    puts = []

    def put(src, dst):
        cp = pltpu.make_async_copy(src, dst, put_sem.at[len(puts)])
        cp.start()
        puts.append(cp)

    got[0].wait()
    got[1].wait()
    for i in range(n):
        rows = pg[i // 2, i % 2].astype(F32) * fac[i : i + 1, 0:1]
        psc[i * run : (i + 1) * run] = rows.astype(BF16)
    for cp in got[2:5]:
        cp.wait()
    tile = 256
    for i in range(width // tile):
        at = slice(i * tile, (i + 1) * tile)
        g2 = dot(tokp[..., at].reshape(tokens, tile), psc[...], 0, 0)
        for h in range(tile // BLK):
            lo = i * tile + h * BLK
            row = mu[lo // BLK : lo // BLK + 1, :] * UNIT
            uo[lo : lo + BLK, :] = (g2[h * BLK : (h + 1) * BLK] * row).astype(BF16)
        put(uo.at[at], up_o.at[at])
    for cp in got[5:]:
        cp.wait()
    put(out_v, out_o)
    put(ing_v, ing_o)
    for i in range(n):
        rows = cotp[i // 2, i % 2].reshape(run, width).astype(F32) * fac[i : i + 1, 0:1]
        csc[i * run : (i + 1) * run] = rows.astype(BF16)
    hf = hid[...].reshape(tokens, hidden)
    for i in range(hidden // tile):
        at = slice(i * tile, (i + 1) * tile)
        g2 = dot(hf[:, at], csc[...], 0, 0)
        for h in range(tile // BLK):
            lo = i * tile + h * BLK
            row = md[lo // BLK : lo // BLK + 1, :] * UNIT
            do[lo : lo + BLK, :] = (g2[h * BLK : (h + 1) * BLK] * row).astype(BF16)
        put(do.at[at], dn_o.at[at])
    for cp in puts:
        cp.wait()


def solution(mesh):
    nz = mesh.shape["row"] // 4
    nc = mesh.shape["col"]

    def local(tok, cot, up, dn, upk, dnk, clip):
        width, hidden = up.shape
        tokens = tok.shape[0] * mesh.shape["row"]
        blk = tokens // nc // 2
        any_, vm, sm = (pl.BlockSpec(memory_space=m) for m in (pl.ANY, pltpu.VMEM, pltpu.SMEM))
        dma = pltpu.SemaphoreType.DMA
        n_ag = 32
        n_row = 2 + len(ROW_KEYS)
        panel = jax.ShapeDtypeStruct((nz, 2, 2, SUB, width), BF16)
        rowed = jax.ShapeDtypeStruct((nz, 2, blk, hidden), BF16)
        shard = jax.ShapeDtypeStruct(tok.shape, BF16)
        up_mask = jax.ShapeDtypeStruct((16, hidden), F32)
        down_mask = jax.ShapeDtypeStruct((8, width), F32)
        factors = jax.ShapeDtypeStruct((2 * nz, BLK), F32)
        made = pl.pallas_call(
            functools.partial(kernel, nz, nc),
            out_shape=(shard, shard, panel, panel, rowed, rowed, up_mask, down_mask, factors),
            in_specs=[any_] * 4 + [sm] * 3,
            out_specs=(any_,) * 9,
            scratch_shapes=[
                pltpu.VMEM(panel.shape, BF16),
                pltpu.VMEM(panel.shape, BF16),
                pltpu.VMEM((width, hidden), BF16),
                pltpu.VMEM((hidden, width), BF16),
                pltpu.VMEM((16, hidden), F32),
                pltpu.VMEM((8, width), F32),
                pltpu.VMEM((4, nc, blk, hidden), BF16),
                pltpu.VMEM((4, nc // 2, blk // 2, hidden), BF16),
                pltpu.VMEM((4, nc // 2, blk // 2, hidden), BF16),
                pltpu.VMEM((4, blk, hidden), BF16),
                pltpu.VMEM((4, nc // 2, blk, hidden), BF16),
                pltpu.VMEM((4, blk // 2, hidden), BF16),
                pltpu.VMEM((4, nc // 2, blk // 2, hidden), BF16),
                pltpu.VMEM(rowed.shape, BF16),
                pltpu.VMEM(rowed.shape, BF16),
                pltpu.VMEM((2, blk, hidden), F32),
                pltpu.VMEM((2, nz, 2, SUB, width), F32),
                pltpu.VMEM((2, nz, 2, SUB, width), F32),
                pltpu.VMEM((2, nz, 2, SUB, width), F32),
                pltpu.VMEM((2, 11, SUB, width), BF16),
                pltpu.VMEM((2, 11, SUB, width), BF16),
                pltpu.VMEM((2, 2, 2, SUB, width), BF16),
                pltpu.VMEM((2, 2, 2, SUB, width), BF16),
                pltpu.VMEM((2, 2, SUB, width), F32),
                pltpu.VMEM((2, SUB, width), BF16),
                pltpu.VMEM((8, BLK), F32),
                pltpu.VMEM((2, 8, BLK), F32),
                pltpu.VMEM((2, 16, 8, BLK), F32),
                pltpu.VMEM((2 * nz, BLK), F32),
                dma((16,)),
                dma((2, n_ag)),
                dma((2, n_ag)),
                dma((8, 14)),
                dma((8, 14)),
                dma((2, n_row)),
                dma((2, n_row)),
                dma((2, 16)),
                dma((2, 16)),
            ],
            compiler_params=pltpu.CompilerParams(
                collective_id=0, has_side_effects=True, vmem_limit_bytes=56 * 1024 * 1024
            ),
        )(tok, cot, up, dn, upk.T, dnk, clip)
        wide = jax.ShapeDtypeStruct((tokens, width), BF16)
        grad_up = jax.ShapeDtypeStruct(up.shape, BF16)
        grad_dn = jax.ShapeDtypeStruct(dn.shape, BF16)
        held = (shard, shard, panel, panel, rowed, rowed, up_mask, down_mask, factors)
        held += (jax.ShapeDtypeStruct((tokens, hidden), BF16), wide, grad_up, grad_dn)
        return pl.pallas_call(
            update,
            out_shape=(shard, shard, grad_up, grad_dn),
            in_specs=[any_] * 9,
            out_specs=(any_,) * 4,
            scratch_shapes=[pltpu.VMEM(t.shape, t.dtype) for t in held] + [dma((16,)), dma((16,))],
            compiler_params=pltpu.CompilerParams(vmem_limit_bytes=60 * 1024 * 1024),
        )(*made)

    placed = (
        P("row", "col"),
        P("row", "col"),
        P("col", "row"),
        P("row", "col"),
        P("col", "row"),
        P("row", "col"),
        P(),
    )
    return jax.shard_map(
        local,
        mesh=mesh,
        in_specs=placed,
        out_specs=(P("row", "col"), P("row", "col"), P("col", "row"), P("row", "col")),
        check_vma=False,
    )
```

time: 98 us -> 100 us (1.020)
  Pallas kernels: 97 us -> 99.4 us
    pallas_call x1, Pallas kernels: 90.6 us -> 93.6 us  [local(): pl.pallas_call(functools.partial(kernel, nz, nc), out_shape=(shard, shard...]
where the time goes in v5:
time: 100 us
  Pallas kernels  99.4 us (99%)
    pallas_call x1, Pallas kernels, local(): pl.pallas_call(functools.partial(kernel, nz, nc), out_shape=(shard, shard...  93.6 us
    pallas_call x1, Pallas kernels, local(): pl.pallas_call(update, out_shape=(shard, shard, grad_up, grad_dn), in_spe...  5.77 us

profile of v5, /device:TPU:1, one launch (start us, length us, event | category | flops | bytes accessed | tf_op | source)
XLA Modules:
  0.0 100.2 jit_solution(6213256893525712288)
XLA Ops:
  0.6 93.6 %shard_map.102 = (bf16[16,1536]{1,0:T(8,128)(2,1)}, bf16[16,1536]{1,0:T(8,128)(2,1)}, bf16[8,2,2,16,1536]{4,3,2,1,0:T(8,128)(2,1)}, bf16[8,2,2,16,1536]{4,3,2,1,...) custom-call(bf16[16,1536]{1,0:T(8,128)(2,1)} %tok.1, ...), custom_call_target="tpu_custom_call" | custom-call | tf_op jit(solution)/shard_map/pallas_call | solution.py:620
  94.3 5.8 %shard_map.103 = (bf16[16,1536]{1,0:T(8,128)(2,1)}, bf16[16,1536]{1,0:T(8,128)(2,1)}, bf16[1536,768]{1,0:T(8,128)(2,1)}, bf16[768,1536]{1,0:T(8,128)(2,1)}) custom-call(bf16[16,1536]{1,0:T(8,128)(2,1)} %get-tuple-element.13.out_t, bf16[16,1536]{1,0:T(8,128)(2,1)} %get-tuple-element.14.ing_t, bf16[8,2,2,16,1536]{4,3,2,1,0:T(8,128)(2,1)} %get-tuple-element.15.tok_t, ...), custom_call_target="tpu_custom_call" | custom-call | tf_op jit(solution)/shard_map/pallas_call | solution.py:674

commit v6 on v5

--- a/solution.py
+++ b/solution.py
@@ -18,7 +18,7 @@
 F32 = jnp.float32
 BF16 = jnp.bfloat16
 ROOT = math.sqrt(2.0 / math.pi)
-ROW_KEYS = [("x", 4), ("x", 3), ("x", -3), ("x", 2), ("x", -2), ("x", 0), ("n", 1), ("n", -1)]
+ROW_KEYS = [("x", 4), ("x", 3), ("x", -3), ("b", 2), ("b", -2), ("x", 0), ("n", 1), ("n", -1)]
 ROW_KEYS += [("r", 4), ("r", 3), ("r", -3), ("z", 2), ("z", -2)]
 UNIT = 7.0 / (EX * math.sqrt(SEQ))
 BOUND = math.sqrt(D * FF * SEQ) / 1000.0
@@ -91,7 +91,13 @@
     own[0].wait()
     own[1].wait()
 
-    pending = []
+    pending, early = [], [0]
+
+    def flush():
+        for copy in pending[: early[0]]:
+            copy.wait_send()
+        del pending[: early[0]]
+        early[0] = len(pending)
 
     def send(src, dst, ssem, rsem, dev):
         copy = pltpu.make_async_remote_copy(
@@ -188,9 +194,6 @@
     gt = Gather(0, tok, tokp)
     gc = Gather(1, cot, cotp)
     gt.start()
-    gt.partner()
-    gt.near()
-    gc.start()
 
     nbu, nbh = width // BLK, hidden // BLK
     for i in range(nbu):
@@ -329,32 +332,40 @@
         g_act[ch].first(0.5 * v * (1.0 + t))
         dact[ch] = 0.5 * (1.0 + t) + (0.5 * ROOT) * v * (1.0 - t * t) * (1.0 + 0.134145 * (v * v))
 
+    gt.partner()
+    gc.start()
+    gt.near()
+    gc.partner()
+    gc.near()
+    gt.far()
+    flush()
     gt.near_done()
     s_pre[NEAR].first(dot(half(tokp, NEAR), upm[...], 1, 0))
-    gt.far()
-    gc.partner()
-    s_pre[NEAR].second()
+    gc.far()
     gt.far_done()
     s_pre[FAR].first(dot(half(tokp, FAR), upm[...], 1, 0))
-    gc.near()
+    s_pre[NEAR].second()
+    flush()
+    gc.near_done()
+    gc.far_done()
+    s_grad[FAR].first(dot(half(cotp, FAR), dnm[...], 1, 1))
+    s_pre[FAR].second()
+    s_grad[NEAR].first(dot(half(cotp, NEAR), dnm[...], 1, 1))
+    flush()
+    activate(NEAR)
+    s_grad[FAR].second()
+    flush()
+    activate(FAR)
+    g_act[NEAR].second()
+    s_grad[NEAR].second()
+    flush()
+    g_pre[FAR].first(s_grad[FAR].total() * dact[FAR])
+    g_act[FAR].second()
+    g_pre[NEAR].first(s_grad[NEAR].total() * dact[NEAR])
     keep(tokp, tok_o, 0)
     keep(mu, mu_o, 1)
     keep(md, md_o, 2)
-    activate(NEAR)
-    s_pre[FAR].second()
-    gc.near_done()
-    gc.far()
-    gc.far_done()
     keep(cotp, cot_o, 3)
-    s_grad[FAR].first(dot(half(cotp, FAR), dnm[...], 1, 1))
-    s_grad[NEAR].first(dot(half(cotp, NEAR), dnm[...], 1, 1))
-    g_act[NEAR].second()
-    activate(FAR)
-    s_grad[FAR].second()
-    s_grad[NEAR].second()
-    g_act[FAR].second()
-    g_pre[FAR].first(s_grad[FAR].total() * dact[FAR])
-    g_pre[NEAR].first(s_grad[NEAR].total() * dact[NEAR])
 
     outs = []
 
@@ -389,11 +400,15 @@
         def get(self, slot, name):
             arrived(row_in.at[self.a, slot], self.key(name)[1], x_dev)
 
-        def along_x(self, slots):
-            for slot in slots:
-                off = (4, 3, -3, 2, -2)[slot]
+        def along_x(self):
+            for slot, off in enumerate((4, 3, -3)):
                 row_out[self.a, slot] = self.q(1, off).astype(BF16)
                 self.out(slot, ("x", off), x_dev)
+
+        def two_on(self, way):
+            off = (2, -2)[way]
+            row_out[self.a, 3 + way] = self.q(1, off).astype(BF16)
+            self.out(3 + way, ("b", off), z_at(off))
 
         def next_door(self):
             for way, sign in ((0, 1), (1, -1)):
@@ -416,16 +431,18 @@
                 val = self.q(m, 0)
                 for way in (0, 1):
                     val += near_in[self.a, way, m].astype(F32)
+                if m == 1:
+                    for way in (0, 1):
+                        self.get(3 + way, ("b", (2, -2)[way]))
+                        val += row_in[self.a, 3 + way].astype(F32)
                 fin[self.a, m] = val
             row_out[self.a, 10] = fin[self.a, 1].astype(BF16)
             self.out(10, ("x", 0), x_dev)
 
         def along_z(self):
             for way, sign in ((0, 1), (1, -1)):
-                self.get(3 + way, ("x", 2 * sign))
                 self.get(6 + way, ("r", 3 * sign))
-                val = self.q(0, 2 * sign) + row_in[self.a, 3 + way].astype(F32)
-                val += row_in[self.a, 6 + way].astype(F32)
+                val = self.q(0, 2 * sign) + row_in[self.a, 6 + way].astype(F32)
                 if way == self.a:
                     self.get(5, ("r", 4))
                     val += row_in[self.a, 5].astype(F32)
@@ -485,26 +502,31 @@
         sq_a[...] = total
 
     ro, ri = RowSum(0), RowSum(1)
+    flush()
     g_act[NEAR].last()
     g_act[FAR].last()
     keep(hid, hid_o, 4)
+    ro.emit(FAR, dot(half(hid, FAR), dnm[...], 1, 0))
     g_pre[FAR].second()
-    ro.emit(FAR, dot(half(hid, FAR), dnm[...], 1, 0))
+    ro.emit(NEAR, dot(half(hid, NEAR), dnm[...], 1, 0))
     g_pre[NEAR].second()
-    ro.emit(NEAR, dot(half(hid, NEAR), dnm[...], 1, 0))
+    ro.pair_wait(FAR)
+    ro.along_x()
+    ro.two_on(1)
+    flush()
     g_pre[FAR].last()
     ri.emit(FAR, dot(half(pg, FAR), upm[...], 1, 1))
-    ro.pair_wait(FAR)
-    ro.along_x((0, 1, 2, 4))
-    ri.pair_wait(FAR)
-    ri.along_x((0, 1, 2, 4))
     ro.pair_wait(NEAR)
-    ro.along_x((3,))
+    ro.two_on(0)
     ro.next_door()
     examples = [(s, h) for s in (0, 1) for h in (0, 1)]
     down_sq = [norm_down(*e) for e in examples]
+    ri.pair_wait(FAR)
+    ri.along_x()
+    ri.two_on(1)
     ro.relay()
 
+    flush()
     g_pre[NEAR].last()
     keep(pg, pg_o, 5)
     ri.emit(NEAR, dot(half(pg, NEAR), upm[...], 1, 1))
@@ -513,16 +535,18 @@
         sq_a[pl.ds(number(*e), 1), :] = jnp.full((1, BLK), norm_up(*e) + down)
     sq_send(0)
     ri.pair_wait(NEAR)
-    ri.along_x((3,))
+    ri.two_on(0)
     ri.next_door()
     ri.relay()
     ro.near()
-    ro.along_z()
+    flush()
     sq_sum(0)
     sq_send(1)
+    ro.along_z()
     ri.near()
     ri.along_z()
     ro.result(out_o, loc_sem.at[4])
+    flush()
     sq_sum(1)
     for p in range(nz):
         for s in (0, 1):

time: 100 us -> 92.9 us (0.929)
  Pallas kernels: 99.4 us -> 91.9 us
    pallas_call x1, Pallas kernels: 93.6 us -> 86.1 us  [local(): pl.pallas_call(functools.partial(kernel, nz, nc), out_shape=(shard, shard...]
where the time goes in v6:
time: 92.9 us; the launch traced here: 92.7 us
  Pallas kernels  91.9 us (99%)
    pallas_call x1, Pallas kernels, local(): pl.pallas_call(functools.partial(kernel, nz, nc), out_shape=(shard, shard...  86.1 us
    pallas_call x1, Pallas kernels, local(): pl.pallas_call(update, out_shape=(shard, shard, grad_up, grad_dn), in_spe...  5.77 us

profile of v6, /device:TPU:1, one launch (start us, length us, event | category | flops | bytes accessed | tf_op | source)
XLA Modules:
  0.0 92.7 jit_solution(16226554559081216916)
XLA Ops:
  0.6 86.1 %shard_map.102 = (bf16[16,1536]{1,0:T(8,128)(2,1)}, bf16[16,1536]{1,0:T(8,128)(2,1)}, bf16[8,2,2,16,1536]{4,3,2,1,0:T(8,128)(2,1)}, bf16[8,2,2,16,1536]{4,3,2,1,...) custom-call(bf16[16,1536]{1,0:T(8,128)(2,1)} %tok.1, ...), custom_call_target="tpu_custom_call" | custom-call | tf_op jit(solution)/shard_map/pallas_call | solution.py:644
  86.8 5.8 %shard_map.103 = (bf16[16,1536]{1,0:T(8,128)(2,1)}, bf16[16,1536]{1,0:T(8,128)(2,1)}, bf16[1536,768]{1,0:T(8,128)(2,1)}, bf16[768,1536]{1,0:T(8,128)(2,1)}) custom-call(bf16[16,1536]{1,0:T(8,128)(2,1)} %get-tuple-element.13.out_t, bf16[16,1536]{1,0:T(8,128)(2,1)} %get-tuple-element.14.ing_t, bf16[8,2,2,16,1536]{4,3,2,1,0:T(8,128)(2,1)} %get-tuple-element.15.tok_t, ...), custom_call_target="tpu_custom_call" | custom-call | tf_op jit(solution)/shard_map/pallas_call | solution.py:698
